TPU v7x, 512 devices: a whole 4x8x8 slice. The times are simulated.
512 devices in a mesh: dp: 32 (over y, z_hi, core), tensor: 16 (over z_lo, x).
Axes of the slice: x: 4, y: 8, z: 8 (z_hi: 2, z_lo: 4; z = z_hi * 4 + z_lo), core: 2. Of those that a mesh axis runs over, the one named last changes fastest.
Arguments:
- act_in: bfloat16 [32768, 28672], P('dp', 'tensor'), may hold values from -6 to 6
- grad_out: bfloat16 [32768, 8192], P('dp', 'tensor'), may hold values from -6 to 6
- proj_in: bfloat16 [28672, 64], P('tensor'), may hold values from -0.015625 to 0.015625
- proj_out: bfloat16 [8192, 64], P('tensor'), may hold values from -0.03125 to 0.03125
- lengths: int32 [1024], P('dp'), may hold values from 1 to 32
- sources: int32 [1024], P('dp'), may hold values from 0 to 255, as said below
- val_feats: bfloat16 [128, 4096], P('dp', 'tensor'), may hold values from -0.046875 to 0.046875
- val_sets: int32 [128, 1], P('dp'), may hold values from 0 to 3
Outputs:
- source_grads: float32 [256, 4096], P('dp', 'tensor')
- pair_scores: float32 [256, 128], P('dp')
- set_scores: float32 [256, 4], P('dp')
Inputs may be any that keep to these rules, and one draw needn't show every extreme that they name: The owner of source c is c // 8. Among the 32 sequences of one index of dp (aligned blocks), at most 2 have sources of one owner, and in every block some owner has exactly 2. `val_sets`: every target set holds at least one validation sequence.
All inputs are finite; a program needn't handle non-finite values.
Results may differ from a plain program's by a relative error of at most 0.0052.
Values may be sent and summed in bfloat16 or wider, within the bound.
No kernel may reach another device: no remote copies, remote signals or barrier semaphores. Data moves between devices by JAX's collectives and lax.ppermute only.
A program may use at most 64 MiB of HBM per device.

v0:
```python
import jax
import jax.numpy as jnp
from jax import lax
from jax.sharding import PartitionSpec as P

SETS = 4
SRC_DEV = 8


def masked_grads(in_proj, out_proj, seq_lengths, seq_count, seq_length):
    live_mask = (jnp.arange(seq_length, dtype=jnp.int32)[None, :] < seq_lengths[:, None]).astype(
        jnp.float32
    )
    in_masked = (in_proj.reshape(seq_count, seq_length, -1) * live_mask[:, :, None]).astype(
        jnp.bfloat16
    )
    out_masked = (out_proj.reshape(seq_count, seq_length, -1) * live_mask[:, :, None]).astype(
        jnp.bfloat16
    )
    grads = jnp.einsum("sta,stb->sab", out_masked, in_masked, preferred_element_type=jnp.float32)
    return grads.reshape(seq_count, -1).astype(jnp.bfloat16)


def place_slots(seq_sources, owner_count, capacity):
    seq_count = seq_sources.shape[0]
    owners = seq_sources // SRC_DEV
    within = seq_sources % SRC_DEV
    shared = owners[:, None] == owners[None, :]
    earlier = jnp.arange(seq_count)[None, :] < jnp.arange(seq_count)[:, None]
    order_in = jnp.sum((shared & earlier).astype(jnp.int32), 1)
    slot_index = owners * capacity + order_in
    placer = (
        jnp.arange(owner_count * capacity, dtype=jnp.int32)[:, None] == slot_index[None, :]
    ).astype(jnp.bfloat16)
    source_tags = jnp.sum(placer.astype(jnp.float32) * (within + 1).astype(jnp.float32)[None, :], 1)
    return (placer, source_tags)


def sum_by_tag(arrived, arrived_tags, feature_count):
    wanted = (jnp.arange(SRC_DEV, dtype=jnp.int32) + 1).astype(jnp.float32)
    chooser = (arrived_tags.reshape(-1).astype(jnp.float32)[None, :] == wanted[:, None]).astype(
        jnp.bfloat16
    )
    return jnp.dot(chooser, arrived.reshape(-1, feature_count), preferred_element_type=jnp.float32)


def local(act_in, grad_out, proj_in, proj_out, lengths, sources, val_feats, val_sets):
    proj_width = proj_in.shape[1]
    seq_count = lengths.shape[0]
    seq_length = act_in.shape[0] // seq_count
    tensor_ranks = lax.axis_size("tensor")
    owner_count = lax.axis_size("dp")
    own_rows = proj_width // tensor_ranks
    feature_count = own_rows * proj_width
    part_in = jnp.dot(act_in, proj_in, preferred_element_type=jnp.float32)
    part_out = jnp.dot(grad_out, proj_out, preferred_element_type=jnp.float32)
    summed = lax.psum(jnp.concatenate([part_in, part_out], 1), "tensor")
    in_proj = summed[:, :proj_width]
    out_proj = lax.dynamic_slice_in_dim(
        summed, proj_width + lax.axis_index("tensor") * own_rows, own_rows, 1
    )
    grads = masked_grads(in_proj, out_proj, lengths, seq_count, seq_length)
    capacity = max(2, (2 * seq_count + owner_count - 1) // owner_count)
    placer, source_tags = place_slots(sources, owner_count, capacity)
    packed = jnp.dot(placer, grads, preferred_element_type=jnp.float32).astype(jnp.bfloat16)
    packed = packed.reshape(owner_count, capacity, feature_count)
    source_tags = source_tags.astype(jnp.bfloat16).reshape(owner_count, capacity)
    arrived, arrived_tags = (
        lax.all_to_all(packed, "dp", split_axis=0, concat_axis=0, tiled=True),
        lax.all_to_all(source_tags, "dp", split_axis=0, concat_axis=0, tiled=True),
    )
    source_grads = sum_by_tag(arrived, arrived_tags, feature_count)
    set_floats = val_sets[:, 0].astype(jnp.bfloat16)
    all_val, all_sets = (
        lax.all_gather(val_feats, "dp", axis=0, tiled=True),
        lax.all_gather(set_floats, "dp", axis=0, tiled=True),
    )
    partial_pair = jnp.dot(
        source_grads, all_val.astype(jnp.float32).T, precision=lax.Precision.HIGHEST
    )
    pair_scores = lax.psum(partial_pair, "tensor")
    set_hot = (
        all_sets.astype(jnp.float32)[:, None]
        == jnp.arange(SETS, dtype=jnp.int32).astype(jnp.float32)[None, :]
    ).astype(jnp.float32)
    set_scores = jnp.dot(pair_scores, set_hot, precision=lax.Precision.HIGHEST) / jnp.sum(
        set_hot, 0
    )
    return (source_grads, pair_scores, set_scores)


def solution(mesh):
    placed = (
        P("dp", "tensor"),
        P("dp", "tensor"),
        P("tensor", None),
        P("tensor", None),
        P("dp"),
        P("dp"),
        P("dp", "tensor"),
        P("dp", None),
    )
    return jax.shard_map(
        local,
        mesh=mesh,
        in_specs=placed,
        out_specs=(P("dp", "tensor"), P("dp", None), P("dp", None)),
        check_vma=False,
    )
```

profile of v0, /device:TPU:8, one launch (start us, length us, event | category | flops | bytes accessed | tf_op | source)
XLA Modules:
  0.0 260.0 jit_solution(2837882817751334026)
XLA Ops:
  7.2 0.0 all-reduce.3.cloned.1.call-start
  7.3 3.3 %fusion.16 = f32[1024,64]{0,1:T(8,128)S(1)} fusion(bf16[1024,1792]{1,0:T(8,128)(2,1)} %param.8, bf16[1792,64]{0,1:T(8,128)(2,1)} %param.10), kind=kOutput, calls=%fused_computation.39 | convolution fusion | flops 234881024 | bytes 4161536 | tf_op jit(solution)/shard_map/dot_general | solution.py:55
  10.6 0.4 fusion.17
  11.1 0.9 pad_maximum_fusion
  11.9 0.0 all-reduce.3.cloned.1.call-update
  12.0 0.2 convert_reduce_fusion.1
  12.2 0.1 multiply_reduce_fusion
  12.3 0.7 convert_element_type.109
  13.0 16.1 %all-to-all-start = ((bf16[32,1,2]{2,1,0:T(2,128)(2,1)}), bf16[32,1,2]{2,1,0:T(2,128)(2,1)S(1)}, u32[]{:S(2)}, u32[]{:S(2)}) async-start(bf16[32,1,2]{2,1,0:T(2,128)(2,1)} %convert_element_type.109), calls=%async_computation | async-start | bytes 32768 | tf_op jit(solution)/shard_map/all_to_all | solution.py:70
  29.2 51.6 %all-gather.1 = bf16[32,4,256]{2,1,0:T(4,128)(2,1)S(1)} all-gather(bf16[1,4,256]{2,1,0:T(4,128)(2,1)S(1)} %bitcast.17), channel_id=1, replica_groups=mesh['dp'=32,'tensor'=16] {'dp'}, dimensions={0}, use_global_device_ids=true | all-gather | bytes 67584 | tf_op jit(solution)/shard_map/all_gather | solution.py:75
  80.9 1.3 dynamic-slice
  82.8 0.2 dynamic-update-slice
  83.0 76.2 %all-reduce = bf16[128]{0:T(256)(128)(2,1)S(1)} all-reduce(bf16[128]{0:T(256)(128)(2,1)S(1)} %dynamic-update-slice), channel_id=2, replica_groups=mesh['dp'=32,'tensor'=16] {'dp'}, use_global_device_ids=true, to_apply=%add | all-reduce | flops 128 | bytes 512
  159.2 0.2 fusion.9
  159.4 0.1 fusion.4
  159.5 24.8 %all-reduce.3.cloned.1.call-done = f32[1024,128]{0,1:T(8,128)} async-done(((f32[1024,128]{0,1:T(8,128)}), f32[1024,128]{0,1:T(8,128)}) %all-reduce.3.cloned.1.call-update) | async-done | bytes 524304 | tf_op jit(solution)/shard_map/psum | solution.py:57
  184.3 0.8 constant_dynamic-slice_fusion
  185.1 0.1 reshape.82
  185.2 1.0 slice.4
  186.1 0.2 copy.18
  186.4 0.3 convolution_convert_fusion.1
  186.7 0.1 convert_element_type.99
  186.8 0.3 convolution_convert_fusion
  187.1 0.6 reshape.84
  187.7 11.4 %all-to-all-start.1 = ((bf16[32,2,256]{2,1,0:T(2,128)(2,1)}), bf16[32,2,256]{2,1,0:T(2,128)(2,1)S(1)}, u32[]{:S(2)}, u32[]{:S(2)}) async-start(bf16[32,2,256]{2,1,0:T(2,128)(2,1)} %reshape.84), calls=%async_computation.1 | async-start | bytes 65536 | tf_op jit(solution)/shard_map/all_to_all | solution.py:69
  199.1 0.1 convert_reduce_fusion
  199.2 0.1 reshape.86
  199.3 11.0 %all-to-all-done.1 = bf16[32,2,256]{2,1,0:T(2,128)(2,1)S(1)} async-done(((bf16[32,2,256]{2,1,0:T(2,128)(2,1)}), bf16[32,2,256]{2,1,0:T(2,128)(2,1)S(1)}, u32[]{:S(2)}, u32[]{:S(2)}) %all-to-all-start.1) | async-done | bytes 32800 | tf_op jit(solution)/shard_map/all_to_all | solution.py:69
  210.3 0.2 fusion.6
  210.5 0.1 fusion.18
  210.6 41.8 %psum.15 = f32[8,128]{1,0:T(8,128)S(1)} all-reduce(f32[8,128]{1,0:T(8,128)S(1)} %fusion.18), channel_id=1, replica_groups=mesh['dp'=32,'tensor'=16] {'tensor'}, use_global_device_ids=true, to_apply=%region_3.4 | all-reduce | flops 1024 | bytes 8192 | tf_op jit(solution)/shard_map/psum | solution.py:81
  252.4 0.8 convolution_divide_fusion
  (27 shorter events, 0.1 us)
Async XLA Ops:
  7.2 3.4 %copy-start = (bf16[1024,512]{1,0:T(8,128)(2,1)S(1)}, bf16[1024,512]{1,0:T(8,128)(2,1)}, u32[]{:S(2)}) copy-start(bf16[1024,512]{1,0:T(8,128)(2,1)} %param.9) | copy-start | bytes 3145732
  7.2 3.4 %copy-start.1 = (bf16[512,64]{0,1:T(8,128)(2,1)S(1)}, bf16[512,64]{0,1:T(8,128)(2,1)}, u32[]{:S(2)}) copy-start(bf16[512,64]{0,1:T(8,128)(2,1)} %param.11) | copy-start | bytes 196612
  7.2 4.8 %copy-start.6 = (s32[32]{0:T(128)S(1)}, s32[32]{0:T(128)}, u32[]{:S(2)}) copy-start(s32[32]{0:T(128)} %param.13) | copy-start | bytes 388
  7.2 22.0 %copy-start.4 = (bf16[4,256]{1,0:T(4,128)(2,1)S(1)}, bf16[4,256]{1,0:T(4,128)(2,1)}, u32[]{:S(2)}) copy-start(bf16[4,256]{1,0:T(4,128)(2,1)} %param.14) | copy-start | bytes 6148
  7.2 73.6 %copy-start.7 = (s32[4,1]{0,1:T(1,128)S(1)}, s32[4,1]{0,1:T(1,128)}, u32[]{:S(2)}) copy-start(s32[4,1]{0,1:T(1,128)} %param.15) | copy-start | bytes 52
  7.2 152.2 %copy-start.5 = (s32[32]{0:T(128)S(1)}, s32[32]{0:T(128)}, u32[]{:S(2)}) copy-start(s32[32]{0:T(128)} %param.12) | copy-start | bytes 388
  7.2 177.1 %all-reduce.3.cloned.1.call-start = ((), (), s32[]{:S(2)}) async-start(), calls=%async_computation.2 | async-start | bytes 1048576 | tf_op jit(solution)/shard_map/psum | solution.py:57
  13.0 174.7 %all-to-all-start = ((bf16[32,1,2]{2,1,0:T(2,128)(2,1)}), bf16[32,1,2]{2,1,0:T(2,128)(2,1)S(1)}, u32[]{:S(2)}, u32[]{:S(2)}) async-start(bf16[32,1,2]{2,1,0:T(2,128)(2,1)} %convert_element_type.109), calls=%async_computation | async-start | bytes 32768 | tf_op jit(solution)/shard_map/all_to_all | solution.py:70
  187.7 22.6 %all-to-all-start.1 = ((bf16[32,2,256]{2,1,0:T(2,128)(2,1)}), bf16[32,2,256]{2,1,0:T(2,128)(2,1)S(1)}, u32[]{:S(2)}, u32[]{:S(2)}) async-start(bf16[32,2,256]{2,1,0:T(2,128)(2,1)} %reshape.84), calls=%async_computation.1 | async-start | bytes 65536 | tf_op jit(solution)/shard_map/all_to_all | solution.py:69
  210.5 42.7 %copy-start.2 = (f32[8,256]{1,0:T(8,128)}, f32[8,256]{1,0:T(8,128)S(1)}, u32[]{:S(2)}) copy-start(f32[8,256]{1,0:T(8,128)S(1)} %fusion.6) | copy-start | bytes 24580
  252.4 0.8 copy-start.3
Sparse Core Ops, SparseCore 0:
  12.1 172.2 all-reduce.2
where the time goes:
time: 260 us
  blocking collectives  170 us (65%)
  waiting for transfers between devices  35.8 us (14%)
  starting transfers between devices  27.6 us (11%)
  between operations  14.9 us (6%)
  matrix products  5.42 us (2%)
  local copies, waits for them, and re-layouts  5.17 us (2%)
    unnamed x1, blocking collectives  76.2 us
    all_gather x1, blocking collectives, local(): lax.all_gather(val_feats, 'dp', axis=0, tiled=True)  51.6 us
    psum x1, blocking collectives, local(): pair_scores = lax.psum(partial_pair, 'tensor')  41.8 us
    psum x1, waiting for transfers between devices, local(): summed = lax.psum(jnp.concatenate([part_in, part_out], 1), 'tensor')  24.8 us
    all_to_all x1, starting transfers between devices, local(): lax.all_to_all(source_tags, 'dp', split_axis=0, concat_axis=0, tiled=True)  16.1 us
    all_to_all x1, starting transfers between devices, local(): lax.all_to_all(packed, 'dp', split_axis=0, concat_axis=0, tiled=True)  11.4 us
    all_to_all x1, waiting for transfers between devices, local(): lax.all_to_all(packed, 'dp', split_axis=0, concat_axis=0, tiled=True)  11 us
  transfers between devices with their start and end apart: 3, of which 2 were waited for; matrix products, arithmetic and copies ran while one was open for 2% of the time, Pallas kernels for 0%

commit v1 on v0

v1 whole, which is shorter than its diff:
```python
import jax
import jax.numpy as jnp
from jax import lax
from jax.sharding import Mesh, PartitionSpec as P

SETS = 4
SRC_DEV = 8
SPLIT = (8, 2, 2, 4, 4)
NAMES = ("y", "h", "c", "z", "x")
DP = ("y", "h", "c")
TENSOR = ("z", "x")
CAP = 2


def exchange(blocks, axes):
    return lax.all_to_all(blocks, axes, 0, 0, tiled=True)


def local(act_in, grad_out, proj_in, proj_out, lengths, sources, val_feats, val_sets):
    bf16, f32, i32 = jnp.bfloat16, jnp.float32, jnp.int32
    width = proj_in.shape[1]
    seqs = lengths.shape[0]
    slots = act_in.shape[0] // seqs
    ranks = lax.axis_size(TENSOR)
    halves = lax.axis_size("h")
    cores = lax.axis_size("c")
    dests = lax.axis_size(("y", "c"))
    mine = seqs // ranks
    feats = width * width // ranks
    rank = lax.axis_index(TENSOR)
    vals = val_feats.shape[0]

    part_in = jnp.dot(act_in, proj_in, preferred_element_type=f32)
    part_out = jnp.dot(grad_out, proj_out, preferred_element_type=f32)
    part = jnp.concatenate([part_in, part_out], 1).astype(bf16)
    part = exchange(part.reshape(ranks, mine * slots, 2 * width), TENSOR)
    whole = jnp.sum(part.astype(f32), 0).reshape(mine, slots, 2 * width)
    live = lax.dynamic_slice_in_dim(lengths, rank * mine, mine)
    mask = jnp.arange(slots, dtype=i32)[None, :] < live[:, None]
    whole = jnp.where(mask[:, :, None], whole, 0.0)
    grads = jnp.einsum(
        "sta,stb->sab",
        whole[:, :, width:],
        whole[:, :, :width],
        precision=lax.Precision.HIGHEST,
        preferred_element_type=f32,
    ).astype(bf16)
    grads = grads.reshape(mine, ranks, feats).transpose(1, 0, 2)

    own = jnp.concatenate([sources.astype(bf16), val_sets[:, 0].astype(bf16)])
    own = jnp.pad(own, (0, feats - own.shape[0]))[None]
    extra = jnp.concatenate([val_feats, own, jnp.zeros((1, feats), bf16)], 0)
    block = jnp.concatenate(
        [grads, jnp.broadcast_to(extra[None], (ranks,) + extra.shape)], 1
    )
    block = jnp.broadcast_to(block[None], (halves,) + block.shape)
    got = exchange(block.reshape((halves * ranks,) + block.shape[2:]), ("h",) + TENSOR)
    got = got.reshape((halves, ranks) + got.shape[1:])
    rows = got[:, :, :mine].reshape(halves * seqs, feats)
    val_rows = lax.dynamic_slice_in_dim(got, rank, 1, 1)[:, 0, mine : mine + vals]
    own_row = got[:, 0, mine + vals]
    source = own_row[:, :seqs].astype(i32)
    set_row = own_row[:, seqs : seqs + vals]

    owner = source // SRC_DEV
    within = source % SRC_DEV
    same = owner[:, :, None] == owner[:, None, :]
    earlier = jnp.arange(seqs)[None, :] < jnp.arange(seqs)[:, None]
    order = jnp.sum((same & earlier[None]).astype(i32), 2)
    dest = owner // (halves * cores) * cores + owner % cores
    slot = (dest * halves + jnp.arange(halves, dtype=i32)[:, None]) * CAP + order
    here = owner // cores % halves == lax.axis_index("h")
    slot = jnp.where(here, slot, -1).reshape(-1)
    placer = jnp.arange(dests * halves * CAP, dtype=i32)[:, None] == slot[None, :]
    packed = jnp.dot(placer.astype(bf16), rows, preferred_element_type=f32).astype(bf16)
    tag = jnp.sum(jnp.where(placer, within.reshape(-1)[None, :] + 1, 0), 1).astype(bf16)
    tag = tag.reshape(dests, 1, halves * CAP)
    packed = packed.reshape(dests, halves * CAP, feats)
    val_all = jnp.broadcast_to(
        val_rows.reshape(1, halves * vals, feats), (dests, halves * vals, feats)
    )
    set_all = jnp.broadcast_to(set_row.reshape(1, 1, -1), (dests, 1, halves * vals))
    told = jnp.concatenate([tag, set_all], 2)
    told = jnp.pad(told, ((0, 0), (0, 3), (0, feats - told.shape[2])))
    came = exchange(jnp.concatenate([packed, val_all, told], 1), ("y", "c"))
    lot = halves * CAP
    arrived = came[:, :lot].reshape(-1, feats)
    tags = came[:, lot + halves * vals, :lot].astype(f32).reshape(-1)
    wanted = (jnp.arange(SRC_DEV, dtype=i32) + 1).astype(f32)
    chooser = (tags[None, :] == wanted[:, None]).astype(bf16)
    source_grads = jnp.dot(chooser, arrived, preferred_element_type=f32)

    def by_dp(a):
        a = a.reshape((-1, cores, halves, vals) + a.shape[2:])
        return jnp.swapaxes(a, 1, 2).reshape((-1,) + a.shape[4:])

    all_val = by_dp(came[:, lot : lot + halves * vals])
    all_sets = by_dp(came[:, lot + halves * vals, lot : lot + halves * vals].astype(f32))
    partial_pair = jnp.dot(
        source_grads, all_val.astype(f32).T, precision=lax.Precision.HIGHEST
    )
    spread = jnp.broadcast_to(partial_pair[None], (ranks,) + partial_pair.shape)
    pair_scores = jnp.sum(exchange(spread, TENSOR), 0)
    set_hot = (all_sets[:, None] == jnp.arange(SETS, dtype=i32).astype(f32)[None, :]).astype(f32)
    set_scores = jnp.dot(pair_scores, set_hot, precision=lax.Precision.HIGHEST) / jnp.sum(set_hot, 0)
    return (source_grads, pair_scores, set_scores)


def solution(mesh):
    parts = Mesh(mesh.devices.reshape(SPLIT), NAMES)
    placed = (
        P(DP, TENSOR),
        P(DP, TENSOR),
        P(TENSOR, None),
        P(TENSOR, None),
        P(DP),
        P(DP),
        P(DP, TENSOR),
        P(DP, None),
    )
    return jax.shard_map(
        local,
        mesh=parts,
        in_specs=placed,
        out_specs=(P(DP, TENSOR), P(DP, None), P(DP, None)),
        check_vma=False,
    )
```

time: 260 us -> 80 us (0.31)
  the two profiles are of different devices: /device:TPU:8 before, /device:TPU:1 now
where the time goes in v1:
time: 80 us; the launch traced here: 79.6 us
  waiting for transfers between devices  34.6 us (43%)
  starting transfers between devices  33 us (41%)
  matrix products  5.36 us (7%)
  local copies, waits for them, and re-layouts  3.01 us (4%)
  other arithmetic  2.64 us (3%)
  between operations  0.95 us (1%)
    all_to_all x4, waiting for transfers between devices, exchange(): return lax.all_to_all(blocks, axes, 0, 0, tiled=True)  34.6 us
    all_to_all x4, starting transfers between devices, exchange(): return lax.all_to_all(blocks, axes, 0, 0, tiled=True)  33 us
    dot_general x1, matrix products, local(): part_in = jnp.dot(act_in, proj_in, preferred_element_type=f32)  3.34 us
  transfers between devices with their start and end apart: 4, of which 4 were waited for; matrix products, arithmetic and copies ran while one was open for 1% of the time, Pallas kernels for 0%

profile of v1, /device:TPU:1, one launch (start us, length us, event | category | flops | bytes accessed | tf_op | source)
XLA Modules:
  0.0 79.6 jit_solution(12634478062798199223)
XLA Ops:
  0.7 3.3 %convolution_convert_fusion.1 = bf16[1024,64]{0,1:T(8,128)(2,1)S(1)} fusion(bf16[1024,1792]{1,0:T(8,128)(2,1)} %param.8, bf16[1792,64]{0,1:T(8,128)(2,1)} %param.10), kind=kOutput, calls=%fused_computation.1 | convolution fusion | flops 234946560 | bytes 4030464 | tf_op jit(solution)/shard_map/dot_general | solution.py:33
  4.0 0.2 copy.40
  4.2 0.4 convolution_convert_fusion
  4.7 0.2 copy.41
  4.9 0.9 %pad_maximum_fusion = bf16[16,64,128]{2,1,0:T(8,128)(2,1)} fusion(bf16[16,64,64]{2,1,0:T(8,128)(2,1)S(1)} %bitcast.26, bf16[16,64,64]{2,1,0:T(8,128)(2,1)S(1)} %bitcast.25), kind=kLoop, calls=%fused_computation.7 | loop fusion | flops 524288 | bytes 524288 | tf_op jit(solution)/shard_map/concatenate | solution.py:35
  5.7 10.4 %all-to-all-start = ((bf16[16,64,128]{2,1,0:T(8,128)(2,1)}), bf16[16,64,128]{2,1,0:T(8,128)(2,1)S(1)}, u32[]{:S(2)}, u32[]{:S(2)}) async-start(bf16[16,64,128]{2,1,0:T(8,128)(2,1)} %pad_maximum_fusion), calls=%async_computation | async-start | bytes 524288 | tf_op jit(solution)/shard_map/all_to_all | solution.py:16
  16.5 9.1 %all-to-all-done = bf16[16,64,128]{2,1,0:T(8,128)(2,1)S(1)} async-done(((bf16[16,64,128]{2,1,0:T(8,128)(2,1)}), bf16[16,64,128]{2,1,0:T(8,128)(2,1)S(1)}, u32[]{:S(2)}, u32[]{:S(2)}) %all-to-all-start) | async-done | bytes 262176 | tf_op jit(solution)/shard_map/all_to_all | solution.py:16
  25.7 0.4 convolution_convert_fusion.3
  26.1 0.1 reshape.127
  26.3 0.6 broadcast_in_dim.49
  26.9 7.7 %all-to-all-start.1 = ((bf16[32,8,256]{2,1,0:T(8,128)(2,1)}), bf16[32,8,256]{2,1,0:T(8,128)(2,1)S(1)}, u32[]{:S(2)}, u32[]{:S(2)}) async-start(bf16[32,8,256]{2,1,0:T(8,128)(2,1)} %bitcast.5), calls=%async_computation.1 | async-start | bytes 262144 | tf_op jit(solution)/shard_map/all_to_all | solution.py:16
  34.7 9.3 %all-to-all-done.1 = bf16[32,8,256]{2,1,0:T(8,128)(2,1)S(1)} async-done(((bf16[32,8,256]{2,1,0:T(8,128)(2,1)}), bf16[32,8,256]{2,1,0:T(8,128)(2,1)S(1)}, u32[]{:S(2)}, u32[]{:S(2)}) %all-to-all-start.1) | async-done | bytes 131104 | tf_op jit(solution)/shard_map/all_to_all | solution.py:16
  44.1 0.2 convert_reduce_fusion.1
  44.3 0.1 eq.75
  44.4 0.1 add.74
  44.5 0.1 select_reduce_fusion
  44.6 0.1 convert_element_type.95
  44.7 0.1 reshape.150
  44.9 0.1 convolution_convert_fusion.2
  45.1 0.7 fusion.1
  45.8 11.4 %all-to-all-start.2 = ((bf16[16,16,256]{2,1,0:T(8,128)(2,1)}), bf16[16,16,256]{2,1,0:T(8,128)(2,1)S(1)}, u32[]{:S(2)}, u32[]{:S(2)}) async-start(bf16[16,16,256]{2,1,0:T(8,128)(2,1)} %fusion.1), calls=%async_computation.2 | async-start | bytes 262144 | tf_op jit(solution)/shard_map/all_to_all | solution.py:16
  57.2 9.2 %all-to-all-done.2 = bf16[16,16,256]{2,1,0:T(8,128)(2,1)S(1)} async-done(((bf16[16,16,256]{2,1,0:T(8,128)(2,1)}), bf16[16,16,256]{2,1,0:T(8,128)(2,1)S(1)}, u32[]{:S(2)}, u32[]{:S(2)}) %all-to-all-start.2) | async-done | bytes 131104 | tf_op jit(solution)/shard_map/all_to_all | solution.py:16
  66.6 0.1 reshape.135
  66.6 0.2 fusion.7
  66.8 0.1 fusion.21
  67.0 0.7 broadcast_in_dim.89
  67.6 3.5 %all-to-all-start.3 = ((f32[16,8,128]{2,1,0:T(8,128)}), f32[16,8,128]{2,1,0:T(8,128)S(1)}, u32[]{:S(2)}, u32[]{:S(2)}) async-start(f32[16,8,128]{2,1,0:T(8,128)} %broadcast_in_dim.89), calls=%async_computation.3 | async-start | bytes 131072 | tf_op jit(solution)/shard_map/all_to_all | solution.py:16
  71.1 0.1 fusion.5
  71.3 0.1 reshape.136
  71.5 0.2 fusion.10
  71.6 7.1 %all-to-all-done.3 = f32[16,8,128]{2,1,0:T(8,128)S(1)} async-done(((f32[16,8,128]{2,1,0:T(8,128)}), f32[16,8,128]{2,1,0:T(8,128)S(1)}, u32[]{:S(2)}, u32[]{:S(2)}) %all-to-all-start.3) | async-done | bytes 65568 | tf_op jit(solution)/shard_map/all_to_all | solution.py:16
  78.8 0.8 convolution_divide_fusion
  (56 shorter events, 1.2 us)
Async XLA Ops:
  0.6 3.6 %copy-start = (bf16[1024,512]{1,0:T(8,128)(2,1)S(1)}, bf16[1024,512]{1,0:T(8,128)(2,1)}, u32[]{:S(2)}) copy-start(bf16[1024,512]{1,0:T(8,128)(2,1)} %param.9) | copy-start | bytes 3145732
  0.6 3.6 %copy-start.1 = (bf16[512,64]{0,1:T(8,128)(2,1)S(1)}, bf16[512,64]{0,1:T(8,128)(2,1)}, u32[]{:S(2)}) copy-start(bf16[512,64]{0,1:T(8,128)(2,1)} %param.11) | copy-start | bytes 196612
  0.7 15.4 %copy-start.5 = (s32[4,1]{0,1:T(1,128)S(1)}, s32[4,1]{0,1:T(1,128)}, u32[]{:S(2)}) copy-start(s32[4,1]{0,1:T(1,128)} %param.15) | copy-start | bytes 52
  0.7 15.5 %copy-start.6 = (s32[32]{0:T(128)S(1)}, s32[32]{0:T(128)}, u32[]{:S(2)}) copy-start(s32[32]{0:T(128)} %param.13) | copy-start | bytes 388
  0.7 15.5 %copy-start.7 = (s32[32]{0:T(128)S(1)}, s32[32]{0:T(128)}, u32[]{:S(2)}) copy-start(s32[32]{0:T(128)} %param.12) | copy-start | bytes 388
  0.7 15.8 %copy-start.4 = (bf16[4,256]{1,0:T(4,128)(2,1)S(1)}, bf16[4,256]{1,0:T(4,128)(2,1)}, u32[]{:S(2)}) copy-start(bf16[4,256]{1,0:T(4,128)(2,1)} %param.14) | copy-start | bytes 6148
  5.7 19.9 %all-to-all-start = ((bf16[16,64,128]{2,1,0:T(8,128)(2,1)}), bf16[16,64,128]{2,1,0:T(8,128)(2,1)S(1)}, u32[]{:S(2)}, u32[]{:S(2)}) async-start(bf16[16,64,128]{2,1,0:T(8,128)(2,1)} %pad_maximum_fusion), calls=%async_computation | async-start | bytes 524288 | tf_op jit(solution)/shard_map/all_to_all | solution.py:16
  26.9 17.1 %all-to-all-start.1 = ((bf16[32,8,256]{2,1,0:T(8,128)(2,1)}), bf16[32,8,256]{2,1,0:T(8,128)(2,1)S(1)}, u32[]{:S(2)}, u32[]{:S(2)}) async-start(bf16[32,8,256]{2,1,0:T(8,128)(2,1)} %bitcast.5), calls=%async_computation.1 | async-start | bytes 262144 | tf_op jit(solution)/shard_map/all_to_all | solution.py:16
  45.8 20.5 %all-to-all-start.2 = ((bf16[16,16,256]{2,1,0:T(8,128)(2,1)}), bf16[16,16,256]{2,1,0:T(8,128)(2,1)S(1)}, u32[]{:S(2)}, u32[]{:S(2)}) async-start(bf16[16,16,256]{2,1,0:T(8,128)(2,1)} %fusion.1), calls=%async_computation.2 | async-start | bytes 262144 | tf_op jit(solution)/shard_map/all_to_all | solution.py:16
  66.8 12.7 %copy-start.2 = (f32[8,256]{1,0:T(8,128)}, f32[8,256]{1,0:T(8,128)S(1)}, u32[]{:S(2)}) copy-start(f32[8,256]{1,0:T(8,128)S(1)} %fusion.7) | copy-start | bytes 24580
  67.6 11.1 %all-to-all-start.3 = ((f32[16,8,128]{2,1,0:T(8,128)}), f32[16,8,128]{2,1,0:T(8,128)S(1)}, u32[]{:S(2)}, u32[]{:S(2)}) async-start(f32[16,8,128]{2,1,0:T(8,128)} %broadcast_in_dim.89), calls=%async_computation.3 | async-start | bytes 131072 | tf_op jit(solution)/shard_map/all_to_all | solution.py:16
  78.8 0.8 copy-start.3

commit v2 on v1

v2 whole, which is shorter than its diff:
```python
import jax
import jax.numpy as jnp
from jax import lax
from jax.experimental import pallas as pl
from jax.experimental.pallas import tpu as pltpu
from jax.sharding import Mesh, PartitionSpec as P

SETS = 4
SRC_DEV = 8
SPLIT = (8, 2, 2, 4, 4)
NAMES = ("y", "h", "c", "z", "x")
DP = ("y", "h", "c")
TENSOR = ("z", "x")
HALVES, CORES, RANKS = 2, 2, 16
DESTS = 16
SEQS, SLOTS, WIDTH = 32, 32, 64
MINE = SEQS // RANKS
FEATS = WIDTH * WIDTH // RANKS
VALS = 4
NVAL = 128
CAP = 2
LOT = HALVES * CAP
NONE = 256.0
PIECES = 2
AT_SOURCE, AT_SET, AT_RANK, AT_HALF, AT_DP = SEQS, 2 * SEQS, 2 * SEQS + VALS, 2 * SEQS + VALS + 1, 2 * SEQS + VALS + 2

bf16, f32, i32 = jnp.bfloat16, jnp.float32, jnp.int32
NT = (((1,), (1,)), ((), ()))
TN = (((0,), (0,)), ((), ()))


def iota(shape, dim):
    return lax.broadcasted_iota(i32, shape, dim)


def project(act_ref, grad_ref, pin_ref, pout_ref, part_ref, act, grad, pin, pout, sems):
    rows = act.shape[0] // PIECES
    moves = [(pin_ref, pin), (pout_ref, pout)]
    for k in range(PIECES):
        cut = pl.ds(k * rows, rows)
        moves += [(act_ref.at[cut], act.at[cut]), (grad_ref.at[cut], grad.at[cut])]
    copies = [pltpu.make_async_copy(*move, sems.at[i]) for i, move in enumerate(moves)]
    for copy in copies:
        copy.start()
    copies[0].wait()
    copies[1].wait()
    for k in range(PIECES):
        cut = pl.ds(k * rows, rows)
        copies[2 + 2 * k].wait()
        copies[3 + 2 * k].wait()
        a = lax.dot_general(pin[...], act[cut, :], NT, preferred_element_type=f32)
        g = lax.dot_general(pout[...], grad[cut, :], NT, preferred_element_type=f32)
        part_ref[cut, :] = jnp.concatenate([a, g], 0).T.astype(bf16)


def gradients(ints, part_ref, val_ref, out_ref, square, tile):
    rank, half = ints[AT_RANK], ints[AT_HALF]
    whole = jnp.sum(part_ref[...].astype(f32), 0)
    flat = []
    for q in range(MINE):
        rows = whole[q * SLOTS : (q + 1) * SLOTS]
        live = iota(rows.shape, 0) < ints[rank * MINE + q]
        rows = jnp.where(live, rows, 0.0)
        square[...] = lax.dot_general(
            rows[:, WIDTH:], rows[:, :WIDTH], TN, precision=lax.Precision.HIGHEST, preferred_element_type=f32
        )
        step = WIDTH // RANKS
        lines = [square[pl.ds(r, RANKS, stride=step), :] for r in range(step)]
        flat.append(jnp.concatenate(lines, 1))

    targets = []
    lane = iota((1, FEATS), 1)
    for q in range(MINE):
        s = rank * MINE + q
        source = ints[AT_SOURCE + s]
        owner = source // SRC_DEV
        order = jnp.int32(0)
        for other in range(SEQS):
            same = (ints[AT_SOURCE + other] // SRC_DEV == owner) & (other < s)
            order = order + same.astype(i32)
        dest = owner // (HALVES * CORES) * CORES + owner % CORES
        slot = dest * 16 + half * CAP + order
        targets.append((owner // CORES % HALVES, slot, source % SRC_DEV + 1))
    sets = jnp.zeros((1, FEATS), f32)
    for r in range(VALS):
        sets = jnp.where(lane == ints[AT_DP] * VALS + r, (ints[AT_SET + r] + 1).astype(f32), sets)
    shape = (RANKS, 8, FEATS)
    row, chunk = iota(shape, 1), iota(shape, 0)
    tile[...] = jnp.zeros(tile.shape, f32)
    tile[2 : 2 + VALS, :] = val_ref[...].astype(f32)
    block = jnp.where(
        chunk == rank,
        jnp.broadcast_to(tile[...][None], shape),
        jnp.where(row == 2, jnp.broadcast_to(sets[None], shape), 0.0),
    )
    for q in range(MINE):
        block = jnp.where(row == q, jnp.broadcast_to(flat[q][:, None, :], shape), block)
    for h in range(HALVES):
        sent = block
        for q in range(MINE):
            to, slot, tag = targets[q]
            slot = jnp.where(to == h, slot, jnp.int32(NONE)).astype(f32)
            told = jnp.where(lane < 128, slot, tag.astype(f32))
            sent = jnp.where(row == 6 + q, jnp.broadcast_to(told[None], shape), sent)
        out_ref[pl.ds(h * RANKS, RANKS)] = sent.astype(bf16)


def pack(ints, got_ref, out_ref):
    rank = ints[AT_RANK]
    x = got_ref[...].astype(f32)
    row, lane = iota(x.shape, 1), iota(x.shape, 2)
    half, j = iota(x.shape, 0) // RANKS, iota(x.shape, 0) % RANKS
    over = lane % 16
    turned = pltpu.roll(x, 2, 1)
    slot = jnp.concatenate([turned[:, :, :128]] * 2, 2).astype(i32)
    told = jnp.concatenate([x[:, :, :128]] * 2, 2).astype(i32)
    val = (j == rank) & (over == LOT + half * VALS + row - 2)
    sets = (j == (rank + 1) % RANKS) & (row == 2) & (over == LOT + HALVES * VALS)
    moves = (
        ((row < 2) & (slot == lane))
        | ((row >= 6) & (told + LOT + HALVES * VALS == lane))
        | ((row >= 2) & (row < 2 + VALS) & (val | sets))
    )
    moves = jnp.where(moves, 1.0, 0.0).reshape(-1, FEATS).astype(bf16)
    x = jnp.where((row >= 6) & (lane < 128), 0.0, x).reshape(-1, FEATS).astype(bf16)
    packed = lax.dot_general(moves, x, TN, preferred_element_type=f32)
    out_ref[...] = packed.astype(bf16).reshape(out_ref.shape)


def score(came_ref, grads_ref, spread_ref, sets_ref):
    x = came_ref[...].astype(f32).reshape(-1, FEATS)
    rows = x.shape[0]
    half = x[:, :128]
    row = iota(half.shape, 0) % 16
    tags = pltpu.roll(x, rows - (LOT + HALVES * VALS), 0)[:, 128:].astype(i32)
    chooser = jnp.where((row < LOT) & (tags == iota(half.shape, 1) + 1), 1.0, 0.0).astype(bf16)
    x = x.astype(bf16)
    source_grads = lax.dot_general(chooser, x, TN, preferred_element_type=f32)[:SRC_DEV]
    grads_ref[...] = source_grads
    sets_ref[...] = jnp.broadcast_to(
        jnp.sum(jnp.where(row == LOT + HALVES * VALS, half, 0.0), 0, keepdims=True), sets_ref.shape
    )
    v, n = iota((NVAL, rows), 0), iota((NVAL, rows), 1)
    r, c, h, y = v % VALS, v // VALS % CORES, v // (VALS * CORES) % HALVES, v // (VALS * CORES * HALVES)
    pick = n == (y * CORES + c) * 16 + LOT + h * VALS + r
    val = jnp.dot(jnp.where(pick, 1.0, 0.0).astype(bf16), x, preferred_element_type=f32)
    pair = lax.dot_general(source_grads, val, NT, precision=lax.Precision.HIGHEST, preferred_element_type=f32)
    spread_ref[...] = jnp.broadcast_to(pair[None], spread_ref.shape)


def finish(parts_ref, sets_ref, pair_ref, set_ref):
    pair = jnp.sum(parts_ref[...], 0)
    pair_ref[...] = pair
    hot = jnp.where(sets_ref[...].astype(i32) == iota(sets_ref.shape, 0) + 1, 1.0, 0.0)
    total = lax.dot_general(hot, pair, NT, precision=lax.Precision.HIGHEST, preferred_element_type=f32)
    set_ref[...] = (total / jnp.sum(hot, 1, keepdims=True))[:SETS]


VMEM = pl.BlockSpec(memory_space=pltpu.VMEM)
SMEM = pl.BlockSpec(memory_space=pltpu.SMEM)
HBM = pl.BlockSpec(memory_space=pltpu.HBM)
PARAMS = pltpu.CompilerParams(vmem_limit_bytes=32 * 2**20)


def here(x):
    return pltpu.with_memory_space_constraint(x, pltpu.VMEM)


def far(x):
    return pltpu.with_memory_space_constraint(x, pltpu.HBM)


def call(kernel, out, specs, scratch=(), **kw):
    return pl.pallas_call(
        kernel,
        out_shape=out,
        in_specs=specs,
        out_specs=jax.tree.map(lambda _: VMEM, out),
        scratch_shapes=scratch,
        compiler_params=PARAMS,
        **kw,
    )


def exchange(blocks, axes):
    return lax.all_to_all(blocks, axes, 0, 0, tiled=True)


def local(act_in, grad_out, proj_in, proj_out, lengths, sources, val_feats, val_sets):
    rows = act_in.shape[0]
    place = jnp.stack([lax.axis_index(TENSOR), lax.axis_index("h"), lax.axis_index(DP)]).astype(i32)
    ints = jnp.concatenate([lengths, sources, val_sets[:, 0], place])
    part = call(
        project,
        pltpu.VMEM((rows, 2 * WIDTH), bf16),
        [HBM] * 4,
        [
            pltpu.VMEM(act_in.shape, bf16),
            pltpu.VMEM(grad_out.shape, bf16),
            pltpu.VMEM(proj_in.shape[::-1], bf16),
            pltpu.VMEM(proj_out.shape[::-1], bf16),
            pltpu.SemaphoreType.DMA((2 + 2 * PIECES,)),
        ],
    )(*(far(x) for x in (act_in, grad_out, proj_in.T, proj_out.T)))
    part = exchange(part.reshape(RANKS, MINE * SLOTS, 2 * WIDTH), TENSOR)
    block = call(
        gradients,
        pltpu.VMEM((HALVES * RANKS, 8, FEATS), bf16),
        [SMEM, VMEM, VMEM],
        [pltpu.VMEM((WIDTH, WIDTH), f32), pltpu.VMEM((8, FEATS), f32)],
    )(ints, here(part), val_feats)
    got = exchange(block, ("h",) + TENSOR)
    packed = call(pack, pltpu.VMEM((DESTS, 16, FEATS), bf16), [SMEM, VMEM])(ints, here(got))
    came = exchange(packed, ("y", "c"))
    source_grads, spread, sets = call(
        score,
        [
            jax.ShapeDtypeStruct((SRC_DEV, FEATS), f32),
            pltpu.VMEM((RANKS, SRC_DEV, NVAL), f32),
            pltpu.VMEM((8, NVAL), f32),
        ],
        [VMEM],
    )(here(came))
    parts = exchange(spread, TENSOR)
    pair_scores, set_scores = call(
        finish,
        [jax.ShapeDtypeStruct((SRC_DEV, NVAL), f32), jax.ShapeDtypeStruct((SETS, SRC_DEV), f32)],
        [VMEM, VMEM],
    )(here(parts), here(sets))
    return (source_grads, pair_scores, set_scores.T)


def solution(mesh):
    parts = Mesh(mesh.devices.reshape(SPLIT), NAMES)
    placed = (
        P(DP, TENSOR),
        P(DP, TENSOR),
        P(TENSOR, None),
        P(TENSOR, None),
        P(DP),
        P(DP),
        P(DP, TENSOR),
        P(DP, None),
    )
    return jax.shard_map(
        local,
        mesh=parts,
        in_specs=placed,
        out_specs=(P(DP, TENSOR), P(DP, None), P(DP, None)),
        check_vma=False,
    )
```

time: 80 us -> 76.3 us (0.954)
  blocking collectives: 0 us -> 47.3 us
  waiting for transfers between devices: 34.6 us -> 9.37 us
  starting transfers between devices: 33 us -> 10.4 us
  Pallas kernels: 0 us -> 8.06 us
  matrix products: 5.36 us -> 0 us
  local copies, waits for them, and re-layouts: 3.01 us -> 0.1 us
  other arithmetic: 2.64 us -> 0 us
    all_to_all x0 -> x3, blocking collectives: none -> 47.3 us  [exchange(): return lax.all_to_all(blocks, axes, 0, 0, tiled=True)]
    all_to_all x4 -> x1, waiting for transfers between devices: 34.6 us -> 9.37 us  [exchange(): return lax.all_to_all(blocks, axes, 0, 0, tiled=True)]
    all_to_all x4 -> x1, starting transfers between devices: 33 us -> 10.4 us  [exchange(): return lax.all_to_all(blocks, axes, 0, 0, tiled=True)]
    pallas_call x0 -> x5, Pallas kernels: none -> 8.06 us  [the longest x1 4.33 us: local(): call(project, pltpu.VMEM((rows, 2 * WIDTH), bf16), [HBM] * 4, [pltpu.VMEM...]
    dot_general x7 -> x0, matrix products: 5.36 us -> none  [the longest x1 3.34 us: local(): part_in = jnp.dot(act_in, proj_in, preferred_element_type=f32)]
    concatenate x6 -> x0, other arithmetic: 1.76 us -> none  [the longest x1 0.85 us: local(): part = jnp.concatenate([part_in, part_out], 1).astype(bf16)]
    broadcast_in_dim x7 -> x0, local copies, waits for them, and re-layouts: 1.46 us -> none  [the longest x1 0.69 us: local(): spread = jnp.broadcast_to(partial_pair[None], (ranks,) + partial_pair.shape)]
  transfers between devices with their start and end apart: 4 -> 1, of which waited for: 4 -> 1; matrix products, arithmetic and copies ran while one was open for 1% -> 0% of each run, Pallas kernels for 0% -> 0%
where the time goes in v2:
time: 76.3 us; the launch traced here: 75.9 us
  blocking collectives  47.3 us (62%)
  starting transfers between devices  10.4 us (14%)
  waiting for transfers between devices  9.37 us (12%)
  Pallas kernels  8.06 us (11%)
    all_to_all x3, blocking collectives, exchange(): return lax.all_to_all(blocks, axes, 0, 0, tiled=True)  47.3 us
    all_to_all x1, starting transfers between devices, exchange(): return lax.all_to_all(blocks, axes, 0, 0, tiled=True)  10.4 us
    all_to_all x1, waiting for transfers between devices, exchange(): return lax.all_to_all(blocks, axes, 0, 0, tiled=True)  9.37 us
    pallas_call x1, Pallas kernels, local(): call(project, pltpu.VMEM((rows, 2 * WIDTH), bf16), [HBM] * 4, [pltpu.VMEM...  4.33 us
  transfers between devices with their start and end apart: 1, of which 1 were waited for; matrix products, arithmetic and copies ran while one was open for 0% of the time, Pallas kernels for 0%

profile of v2, /device:TPU:1, one launch (start us, length us, event | category | flops | bytes accessed | tf_op | source)
XLA Modules:
  0.0 75.9 jit_solution(7847427724343771965)
XLA Ops:
  0.6 0.0 copy-start.3
  0.6 0.0 copy-start.2
  0.7 0.0 copy-start.1
  0.7 0.0 copy-start
  0.7 4.3 %shard_map.103 = bf16[1024,128]{1,0:T(8,128)(2,1)} custom-call(bf16[1024,1792]{1,0:T(8,128)(2,1)} %act_ref.1, bf16[1024,512]{1,0:T(8,128)(2,1)} %grad_ref.1, bf16[64,1792]{1,0:T(8,128)(2,1)} %bitcast.8, bf16[64,512]{1,0:T(8,128)(2,1)} %bitcast.9), custom_call_target="tpu_custom_call" | custom-call | tf_op jit(solution)/shard_map/pallas_call | solution.py:193
  5.0 10.4 %all-to-all-start = ((bf16[16,64,128]{2,1,0:T(8,128)(2,1)}), bf16[16,64,128]{2,1,0:T(8,128)(2,1)S(1)}, u32[]{:S(2)}, u32[]{:S(2)}) async-start(bf16[16,64,128]{2,1,0:T(8,128)(2,1)} %bitcast.6), calls=%async_computation | async-start | bytes 524288 | tf_op jit(solution)/shard_map/all_to_all | solution.py:186
  15.4 0.0 copy-done.3
  15.4 0.0 copy-done.2
  15.4 0.0 copy-done.1
  15.4 0.1 concatenate.3.ints
  15.5 9.4 %all-to-all-done.part_ref = bf16[16,64,128]{2,1,0:T(8,128)(2,1)S(1)} async-done(((bf16[16,64,128]{2,1,0:T(8,128)(2,1)}), bf16[16,64,128]{2,1,0:T(8,128)(2,1)S(1)}, u32[]{:S(2)}, u32[]{:S(2)}) %all-to-all-start) | async-done | bytes 262176 | tf_op jit(solution)/shard_map/all_to_all | solution.py:186
  24.9 0.0 copy-done
  24.9 1.2 %shard_map.104 = bf16[32,8,256]{2,1,0:T(8,128)(2,1)S(1)} custom-call(s32[71]{0:T(128)S(1)} %concatenate.3.ints, bf16[16,64,128]{2,1,0:T(8,128)(2,1)S(1)} %all-to-all-done.part_ref, bf16[4,256]{1,0:T(4,128)(2,1)S(1)} %copy-done), custom_call_target="tpu_custom_call" | custom-call | tf_op jit(solution)/shard_map/pallas_call | solution.py:206
  26.1 16.9 %all_to_all.20.got_ref = bf16[32,8,256]{2,1,0:T(8,128)(2,1)S(1)} all-to-all(bf16[32,8,256]{2,1,0:T(8,128)(2,1)S(1)} %shard_map.104), channel_id=1, replica_groups=mesh['y'=8,'h'=2,'c'=2,'z'=4,'x'=4] {'h','z','x'}, dimensions={0} | all-to-all | bytes 262144 | tf_op jit(solution)/shard_map/all_to_all | solution.py:186
  42.9 1.1 %shard_map.105 = bf16[16,16,256]{2,1,0:T(8,128)(2,1)S(1)} custom-call(s32[71]{0:T(128)S(1)} %concatenate.3.ints, bf16[32,8,256]{2,1,0:T(8,128)(2,1)S(1)} %all_to_all.20.got_ref), custom_call_target="tpu_custom_call" | custom-call | tf_op jit(solution)/shard_map/pallas_call | solution.py:213
  44.0 20.3 %all_to_all.21.came_ref = bf16[16,16,256]{2,1,0:T(8,128)(2,1)S(1)} all-to-all(bf16[16,16,256]{2,1,0:T(8,128)(2,1)S(1)} %shard_map.105), channel_id=1, replica_groups=mesh['y'=8,'h'=2,'c'=2,'z'=4,'x'=4] {'y','c'}, dimensions={0} | all-to-all | bytes 262144 | tf_op jit(solution)/shard_map/all_to_all | solution.py:186
  64.3 0.8 %shard_map.106 = (f32[8,256]{1,0:T(8,128)}, f32[16,8,128]{2,1,0:T(8,128)S(1)}, f32[8,128]{1,0:T(8,128)S(1)}) custom-call(bf16[16,16,256]{2,1,0:T(8,128)(2,1)S(1)} %all_to_all.21.came_ref), custom_call_target="tpu_custom_call" | custom-call | tf_op jit(solution)/shard_map/pallas_call | solution.py:215
  65.1 10.1 %all_to_all.22.parts_ref = f32[16,8,128]{2,1,0:T(8,128)S(1)} all-to-all(f32[16,8,128]{2,1,0:T(8,128)S(1)} %get-tuple-element.9), channel_id=1, replica_groups=mesh['y'=8,'h'=2,'c'=2,'z'=4,'x'=4] {'z','x'}, dimensions={0} | all-to-all | bytes 131072 | tf_op jit(solution)/shard_map/all_to_all | solution.py:186
  75.2 0.7 shard_map.107
Async XLA Ops:
  0.6 14.8 %copy-start.3 = (s32[4,1]{0,1:T(1,128)S(1)}, s32[4,1]{0,1:T(1,128)}, u32[]{:S(2)}) copy-start(s32[4,1]{0,1:T(1,128)} %param.15) | copy-start | bytes 52
  0.6 14.8 %copy-start.2 = (s32[32]{0:T(128)S(1)}, s32[32]{0:T(128)}, u32[]{:S(2)}) copy-start(s32[32]{0:T(128)} %param.13) | copy-start | bytes 388
  0.7 14.8 %copy-start.1 = (s32[32]{0:T(128)S(1)}, s32[32]{0:T(128)}, u32[]{:S(2)}) copy-start(s32[32]{0:T(128)} %param.12) | copy-start | bytes 388
  0.7 24.2 %copy-start = (bf16[4,256]{1,0:T(4,128)(2,1)S(1)}, bf16[4,256]{1,0:T(4,128)(2,1)}, u32[]{:S(2)}) copy-start(bf16[4,256]{1,0:T(4,128)(2,1)} %val_ref.1) | copy-start | bytes 6148
  5.0 19.9 %all-to-all-start = ((bf16[16,64,128]{2,1,0:T(8,128)(2,1)}), bf16[16,64,128]{2,1,0:T(8,128)(2,1)S(1)}, u32[]{:S(2)}, u32[]{:S(2)}) async-start(bf16[16,64,128]{2,1,0:T(8,128)(2,1)} %bitcast.6), calls=%async_computation | async-start | bytes 524288 | tf_op jit(solution)/shard_map/all_to_all | solution.py:186

commit v3 on v2

v3 whole, which is shorter than its diff:
```python
import jax
import jax.numpy as jnp
from jax import lax
from jax.experimental import pallas as pl
from jax.experimental.pallas import tpu as pltpu
from jax.sharding import Mesh, PartitionSpec as P

SETS = 4
SRC_DEV = 8
SPLIT = (8, 2, 2, 4, 4)
NAMES = ("y", "h", "c", "z", "x")
DP = ("y", "h", "c")
TENSOR = ("z", "x")
HALVES, CORES, RANKS = 2, 2, 16
DESTS = 16
SEQS, SLOTS, WIDTH = 32, 32, 64
MINE = SEQS // RANKS
FEATS = WIDTH * WIDTH // RANKS
VALS = 4
NVAL = 128
CAP = 2
LOT = HALVES * CAP
NONE = 256.0
PIECES = 2
bf16, f32, i32 = jnp.bfloat16, jnp.float32, jnp.int32
NT = (((1,), (1,)), ((), ()))
TN = (((0,), (0,)), ((), ()))


def iota(shape, dim):
    return lax.broadcasted_iota(i32, shape, dim)


def tell(lengths, sources, sets, val, live_ref, base_ref, lay_ref):
    rank, half, dp = lax.axis_index(TENSOR), lax.axis_index("h"), lax.axis_index(DP)
    for q in range(MINE):
        cut = pl.ds(q * SLOTS, SLOTS)
        shape = (SLOTS, 2 * WIDTH)
        live_ref[cut, :] = jnp.where(iota(shape, 0) < lengths[rank * MINE + q], 1.0, 0.0)
    lane = iota((1, FEATS), 1)
    marks = jnp.zeros((1, FEATS), f32)
    for r in range(VALS):
        marks = jnp.where(lane == dp * VALS + r, (sets[0, r] + 1).astype(f32), marks)
    told = []
    for q in range(MINE):
        s = rank * MINE + q
        source = sources[s]
        owner = source // SRC_DEV
        order = jnp.int32(0)
        for other in range(SEQS):
            same = (sources[other] // SRC_DEV == owner) & (other < s)
            order = order + same.astype(i32)
        dest = owner // (HALVES * CORES) * CORES + owner % CORES
        told.append((owner // CORES % HALVES, dest * 16 + half * CAP + order, source % SRC_DEV + 1))
    shape = (RANKS, 8, FEATS)
    row, chunk = iota(shape, 1), iota(shape, 0)
    over = iota(shape, 2) % 16
    base_ref[0] = jnp.zeros((8, FEATS), f32)
    base_ref[0, 2 : 2 + VALS, :] = val[...].astype(f32)
    rows = jnp.broadcast_to(base_ref[0][None], shape)
    rows = jnp.where(chunk == rank, rows, jnp.where(row == 2, jnp.broadcast_to(marks[None], shape), 0.0))
    for h in range(HALVES):
        sent = rows
        for q in range(MINE):
            to, slot, tag = told[q]
            slot = jnp.where(to == h, slot, jnp.int32(NONE)).astype(f32)
            line = jnp.where(lane < 128, slot, tag.astype(f32))
            sent = jnp.where(row == 6 + q, jnp.broadcast_to(line[None], shape), sent)
        base_ref[pl.ds(h * RANKS, RANKS)] = sent
        is_val = (chunk == rank) & (over == LOT + h * VALS + row - 2)
        is_set = (chunk == (rank + 1) % RANKS) & (row == 2) & (over == LOT + HALVES * VALS)
        lay = (row >= 2) & (row < 2 + VALS) & (is_val | is_set)
        lay_ref[pl.ds(h * RANKS, RANKS)] = jnp.where(lay, 1.0, 0.0)


def project(*refs):
    sources, (part_ref, live_ref, base_ref, lay_ref), held, sems = refs[:8], refs[8:12], refs[12:20], refs[20]
    act, grad, pin, pout, lengths, owners, sets, val = held
    rows = act.shape[0] // PIECES
    moves = list(zip(sources[2:], held[2:]))
    for k in range(PIECES):
        cut = pl.ds(k * rows, rows)
        moves += [(sources[0].at[cut], act.at[cut]), (sources[1].at[cut], grad.at[cut])]
    copies = [pltpu.make_async_copy(*move, sems.at[i]) for i, move in enumerate(moves)]
    for copy in copies:
        copy.start()
    for copy in copies[2:6]:
        copy.wait()
    tell(lengths, owners, sets, val, live_ref, base_ref, lay_ref)
    copies[0].wait()
    copies[1].wait()
    for k in range(PIECES):
        cut = pl.ds(k * rows, rows)
        copies[6 + 2 * k].wait()
        copies[7 + 2 * k].wait()
        a = lax.dot_general(pin[...], act[cut, :], NT, preferred_element_type=f32)
        g = lax.dot_general(pout[...], grad[cut, :], NT, preferred_element_type=f32)
        part_ref[cut, :] = jnp.concatenate([a, g], 0).T.astype(bf16)


def gradients(part_ref, live_ref, base_ref, out_ref, square):
    whole = jnp.sum(part_ref[...].astype(f32), 0)
    whole = jnp.where(live_ref[...] > 0.0, whole, 0.0)
    flat = []
    for q in range(MINE):
        rows = whole[q * SLOTS : (q + 1) * SLOTS]
        square[q] = lax.dot_general(
            rows[:, WIDTH:], rows[:, :WIDTH], TN, precision=lax.Precision.HIGHEST, preferred_element_type=f32
        )
        step = WIDTH // RANKS
        lines = [square[q, pl.ds(r, RANKS, stride=step), :] for r in range(step)]
        flat.append(jnp.concatenate(lines, 1))
    shape = (RANKS, 8, FEATS)
    row = iota(shape, 1)
    for h in range(HALVES):
        cut = pl.ds(h * RANKS, RANKS)
        sent = base_ref[cut]
        for q in range(MINE):
            sent = jnp.where(row == q, jnp.broadcast_to(flat[q][:, None, :], shape), sent)
        out_ref[cut] = sent.astype(bf16)


def pack(got_ref, lay_ref, out_ref):
    x = got_ref[...].astype(f32)
    row, lane = iota(x.shape, 1), iota(x.shape, 2)
    turned = pltpu.roll(x, 2, 1)
    slot = jnp.concatenate([turned[:, :, :128]] * 2, 2).astype(i32)
    told = jnp.concatenate([x[:, :, :128]] * 2, 2).astype(i32)
    moves = ((row < 2) & (slot == lane)) | ((row >= 6) & (told + LOT + HALVES * VALS == lane))
    moves = jnp.where(moves, 1.0, lay_ref[...]).reshape(-1, FEATS).astype(bf16)
    x = jnp.where((row >= 6) & (lane < 128), 0.0, x).reshape(-1, FEATS).astype(bf16)
    packed = lax.dot_general(moves, x, TN, preferred_element_type=f32)
    out_ref[...] = packed.astype(bf16).reshape(out_ref.shape)


def score(came_ref, grads_ref, spread_ref, sets_ref):
    x = came_ref[...].astype(f32).reshape(-1, FEATS)
    rows = x.shape[0]
    half = x[:, :128]
    row = iota(half.shape, 0) % 16
    tags = pltpu.roll(x, rows - (LOT + HALVES * VALS), 0)[:, 128:].astype(i32)
    chooser = jnp.where((row < LOT) & (tags == iota(half.shape, 1) + 1), 1.0, 0.0).astype(bf16)
    x = x.astype(bf16)
    source_grads = lax.dot_general(chooser, x, TN, preferred_element_type=f32)[:SRC_DEV]
    grads_ref[...] = source_grads
    sets_ref[...] = jnp.broadcast_to(
        jnp.sum(jnp.where(row == LOT + HALVES * VALS, half, 0.0), 0, keepdims=True), sets_ref.shape
    )
    v, n = iota((NVAL, rows), 0), iota((NVAL, rows), 1)
    r, c, h, y = v % VALS, v // VALS % CORES, v // (VALS * CORES) % HALVES, v // (VALS * CORES * HALVES)
    pick = n == (y * CORES + c) * 16 + LOT + h * VALS + r
    val = jnp.dot(jnp.where(pick, 1.0, 0.0).astype(bf16), x, preferred_element_type=f32)
    pair = lax.dot_general(source_grads, val, NT, precision=lax.Precision.HIGHEST, preferred_element_type=f32)
    spread_ref[...] = jnp.broadcast_to(pair[None], spread_ref.shape)


def finish(parts_ref, sets_ref, grads_ref, pair_ref, set_ref, out_ref):
    out_ref[...] = grads_ref[...]
    pair = jnp.sum(parts_ref[...], 0)
    pair_ref[...] = pair
    hot = jnp.where(sets_ref[...].astype(i32) == iota(sets_ref.shape, 0) + 1, 1.0, 0.0)
    total = lax.dot_general(hot, pair, NT, precision=lax.Precision.HIGHEST, preferred_element_type=f32)
    set_ref[...] = (total / jnp.sum(hot, 1, keepdims=True))[:SETS]


VMEM = pl.BlockSpec(memory_space=pltpu.VMEM)
HBM = pl.BlockSpec(memory_space=pltpu.HBM)
PARAMS = pltpu.CompilerParams(vmem_limit_bytes=32 * 2**20)


def here(x):
    return pltpu.with_memory_space_constraint(x, pltpu.VMEM)


def far(x):
    return pltpu.with_memory_space_constraint(x, pltpu.HBM)


def call(kernel, out, specs, scratch=(), **kw):
    return pl.pallas_call(
        kernel,
        out_shape=out,
        in_specs=specs,
        out_specs=jax.tree.map(lambda _: VMEM, out),
        scratch_shapes=scratch,
        compiler_params=PARAMS,
        **kw,
    )


def exchange(blocks, axes):
    return lax.all_to_all(blocks, axes, 0, 0, tiled=True)


def local(act_in, grad_out, proj_in, proj_out, lengths, sources, val_feats, val_sets):
    rows = act_in.shape[0]
    chunks = (HALVES * RANKS, 8, FEATS)
    args = (act_in, grad_out, proj_in.T, proj_out.T, lengths, sources, val_sets.T, val_feats)
    homes = [pltpu.VMEM] * 4 + [pltpu.SMEM] * 3 + [pltpu.VMEM]
    part, live, base, lay = call(
        project,
        [
            pltpu.VMEM((rows, 2 * WIDTH), bf16),
            pltpu.VMEM((MINE * SLOTS, 2 * WIDTH), f32),
            pltpu.VMEM(chunks, f32),
            pltpu.VMEM(chunks, f32),
        ],
        [HBM] * 8,
        [home(x.shape, x.dtype) for home, x in zip(homes, args)] + [pltpu.SemaphoreType.DMA((6 + 2 * PIECES,))],
    )(*(far(x) for x in args))
    part = exchange(part.reshape(RANKS, MINE * SLOTS, 2 * WIDTH), TENSOR)
    block = call(gradients, pltpu.VMEM(chunks, bf16), [VMEM] * 3, [pltpu.VMEM((MINE, WIDTH, WIDTH), f32)])(
        here(part), here(live), here(base)
    )
    got = exchange(block, ("h",) + TENSOR)
    packed = call(pack, pltpu.VMEM((DESTS, 16, FEATS), bf16), [VMEM] * 2)(here(got), here(lay))
    came = exchange(packed, ("y", "c"))
    source_grads, spread, sets = call(
        score,
        [
            pltpu.VMEM((SRC_DEV, FEATS), f32),
            pltpu.VMEM((RANKS, SRC_DEV, NVAL), f32),
            pltpu.VMEM((8, NVAL), f32),
        ],
        [VMEM],
    )(here(came))
    parts = exchange(spread, TENSOR)
    pair_scores, set_scores, source_grads = call(
        finish,
        [
            jax.ShapeDtypeStruct((SRC_DEV, NVAL), f32),
            jax.ShapeDtypeStruct((SETS, SRC_DEV), f32),
            jax.ShapeDtypeStruct((SRC_DEV, FEATS), f32),
        ],
        [VMEM] * 3,
    )(here(parts), here(sets), here(source_grads))
    return (source_grads, pair_scores, set_scores.T)


def solution(mesh):
    parts = Mesh(mesh.devices.reshape(SPLIT), NAMES)
    placed = (
        P(DP, TENSOR),
        P(DP, TENSOR),
        P(TENSOR, None),
        P(TENSOR, None),
        P(DP),
        P(DP),
        P(DP, TENSOR),
        P(DP, None),
    )
    return jax.shard_map(
        local,
        mesh=parts,
        in_specs=placed,
        out_specs=(P(DP, TENSOR), P(DP, None), P(DP, None)),
        check_vma=False,
    )
```

time: 76.3 us -> 73.5 us (0.963)
  blocking collectives: 47.3 us -> 67 us
  starting transfers between devices: 10.4 us -> 0 us
  waiting for transfers between devices: 9.37 us -> 0 us
  Pallas kernels: 8.06 us -> 5.59 us
    all_to_all x3 -> x4, blocking collectives: 47.3 us -> 67 us  [exchange(): return lax.all_to_all(blocks, axes, 0, 0, tiled=True)]
    all_to_all x1 -> x0, starting transfers between devices: 10.4 us -> none  [exchange(): return lax.all_to_all(blocks, axes, 0, 0, tiled=True)]
    all_to_all x1 -> x0, waiting for transfers between devices: 9.37 us -> none  [exchange(): return lax.all_to_all(blocks, axes, 0, 0, tiled=True)]
    pallas_call x4, Pallas kernels: 7.34 us -> 4.85 us  [the longest x1 3.66 us: local(): call(project, [pltpu.VMEM((rows, 2 * WIDTH), bf16), pltpu.VMEM((MINE * SL...]
  transfers between devices with their start and end apart: 1 -> 0, of which waited for: 1 -> 0; matrix products, arithmetic and copies ran while one was open for 0% -> 0% of each run, Pallas kernels for 0% -> 0%
where the time goes in v3:
time: 73.5 us; the launch traced here: 73.3 us
  blocking collectives  67 us (91%)
  Pallas kernels  5.59 us (8%)
    all_to_all x4, blocking collectives, exchange(): return lax.all_to_all(blocks, axes, 0, 0, tiled=True)  67 us
    pallas_call x1, Pallas kernels, local(): call(project, [pltpu.VMEM((rows, 2 * WIDTH), bf16), pltpu.VMEM((MINE * SL...  3.66 us

profile of v3, /device:TPU:1, one launch (start us, length us, event | category | flops | bytes accessed | tf_op | source)
XLA Modules:
  0.0 73.3 jit_solution(10586434574867925452)
XLA Ops:
  0.6 3.7 %shard_map.103 = (bf16[1024,128]{1,0:T(8,128)(2,1)S(1)}, f32[64,128]{1,0:T(8,128)S(1)}, f32[32,8,256]{2,1,0:T(8,128)S(1)}, f32[32,8,256]{2,1,0:T(8,128)S(1)}) custom-call(bf16[1024,1792]{1,0:T(8,128)(2,1)} %refs_0_.1, bf16[1024,512]{1,0:T(8,128)(2,1)} %refs_1_.1, bf16[64,1792]{1,0:T(8,128)(2,1)} %bitcast.6, bf16[64,512]{1,0:T(8,128)(2,1)} %bitcast.7, ...), custom_call_target="tpu_custom_call" | custom-call | tf_op jit(solution)/shard_map/pallas_call | solution.py:200
  4.3 19.7 %all_to_all.20.part_ref = bf16[16,64,128]{2,1,0:T(8,128)(2,1)S(1)} all-to-all(bf16[16,64,128]{2,1,0:T(8,128)(2,1)S(1)} %bitcast.5), channel_id=1, replica_groups=mesh['y'=8,'h'=2,'c'=2,'z'=4,'x'=4] {'z','x'}, dimensions={0} | all-to-all | bytes 524288 | tf_op jit(solution)/shard_map/all_to_all | solution.py:192
  24.0 0.5 shard_map.104
  24.5 16.9 %all_to_all.21.got_ref = bf16[32,8,256]{2,1,0:T(8,128)(2,1)S(1)} all-to-all(bf16[32,8,256]{2,1,0:T(8,128)(2,1)S(1)} %shard_map.104), channel_id=1, replica_groups=mesh['y'=8,'h'=2,'c'=2,'z'=4,'x'=4] {'h','z','x'}, dimensions={0} | all-to-all | bytes 262144 | tf_op jit(solution)/shard_map/all_to_all | solution.py:192
  41.3 0.3 shard_map.105
  41.6 20.3 %all_to_all.22.came_ref = bf16[16,16,256]{2,1,0:T(8,128)(2,1)S(1)} all-to-all(bf16[16,16,256]{2,1,0:T(8,128)(2,1)S(1)} %shard_map.105), channel_id=1, replica_groups=mesh['y'=8,'h'=2,'c'=2,'z'=4,'x'=4] {'y','c'}, dimensions={0} | all-to-all | bytes 262144 | tf_op jit(solution)/shard_map/all_to_all | solution.py:192
  62.0 0.4 shard_map.106
  62.4 10.2 %all_to_all.23.parts_ref = f32[16,8,128]{2,1,0:T(8,128)S(1)} all-to-all(f32[16,8,128]{2,1,0:T(8,128)S(1)} %get-tuple-element.17), channel_id=1, replica_groups=mesh['y'=8,'h'=2,'c'=2,'z'=4,'x'=4] {'z','x'}, dimensions={0} | all-to-all | bytes 131072 | tf_op jit(solution)/shard_map/all_to_all | solution.py:192
  72.5 0.7 %shard_map.107 = (f32[8,128]{1,0:T(8,128)}, f32[4,8]{1,0:T(4,128)}, f32[8,256]{1,0:T(8,128)}) custom-call(f32[16,8,128]{2,1,0:T(8,128)S(1)} %all_to_all.23.parts_ref, f32[8,128]{1,0:T(8,128)S(1)} %get-tuple-element.18.sets_ref, f32[8,256]{1,0:T(8,128)S(1)} %get-tuple-element.19.grads_ref), custom_call_target="tpu_custom_call" | custom-call | tf_op jit(solution)/shard_map/pallas_call | solution.py:228

commit v4 on v3

--- a/solution.py
+++ b/solution.py
@@ -21,7 +21,7 @@
 CAP = 2
 LOT = HALVES * CAP
 NONE = 256.0
-PIECES = 2
+CUTS = (0, 256, 512, 1024, 1536, 1792)
 bf16, f32, i32 = jnp.bfloat16, jnp.float32, jnp.int32
 NT = (((1,), (1,)), ((), ()))
 TN = (((0,), (0,)), ((), ()))
@@ -34,9 +34,8 @@
 def tell(lengths, sources, sets, val, live_ref, base_ref, lay_ref):
     rank, half, dp = lax.axis_index(TENSOR), lax.axis_index("h"), lax.axis_index(DP)
     for q in range(MINE):
-        cut = pl.ds(q * SLOTS, SLOTS)
-        shape = (SLOTS, 2 * WIDTH)
-        live_ref[cut, :] = jnp.where(iota(shape, 0) < lengths[rank * MINE + q], 1.0, 0.0)
+        slot = iota((WIDTH, 2 * WIDTH), 1) - q * SLOTS
+        live_ref[q] = jnp.where((slot >= 0) & (slot < lengths[rank * MINE + q]), 1.0, 0.0)
     lane = iota((1, FEATS), 1)
     marks = jnp.zeros((1, FEATS), f32)
     for r in range(VALS):
@@ -76,36 +75,41 @@
 def project(*refs):
     sources, (part_ref, live_ref, base_ref, lay_ref), held, sems = refs[:8], refs[8:12], refs[12:20], refs[20]
     act, grad, pin, pout, lengths, owners, sets, val = held
-    rows = act.shape[0] // PIECES
-    moves = list(zip(sources[2:], held[2:]))
-    for k in range(PIECES):
-        cut = pl.ds(k * rows, rows)
-        moves += [(sources[0].at[cut], act.at[cut]), (sources[1].at[cut], grad.at[cut])]
+    moves = [(sources[i], held[i]) for i in (4, 5, 6, 7, 3, 1, 2)]
+    cuts = [pl.ds(lo, hi - lo) for lo, hi in zip(CUTS[:-1], CUTS[1:])]
+    moves += [(sources[0].at[:, cut], act.at[:, cut]) for cut in cuts]
     copies = [pltpu.make_async_copy(*move, sems.at[i]) for i, move in enumerate(moves)]
     for copy in copies:
         copy.start()
-    for copy in copies[2:6]:
+    for copy in copies[:4]:
         copy.wait()
     tell(lengths, owners, sets, val, live_ref, base_ref, lay_ref)
-    copies[0].wait()
-    copies[1].wait()
-    for k in range(PIECES):
-        cut = pl.ds(k * rows, rows)
-        copies[6 + 2 * k].wait()
-        copies[7 + 2 * k].wait()
-        a = lax.dot_general(pin[...], act[cut, :], NT, preferred_element_type=f32)
-        g = lax.dot_general(pout[...], grad[cut, :], NT, preferred_element_type=f32)
-        part_ref[cut, :] = jnp.concatenate([a, g], 0).T.astype(bf16)
+    copies[4].wait()
+    copies[5].wait()
+    out = lax.dot_general(pout[...], grad[...], NT, preferred_element_type=f32)
+    copies[6].wait()
+    total = None
+    for cut, copy in zip(cuts, copies[7:]):
+        copy.wait()
+        term = lax.dot_general(pin[:, cut], act[:, cut], NT, preferred_element_type=f32)
+        total = term if total is None else total + term
+    tokens = MINE * SLOTS
+    for j in range(RANKS):
+        cut = slice(j * tokens, (j + 1) * tokens)
+        part_ref[j] = jnp.concatenate([total[:, cut], out[:, cut]], 1).astype(bf16)
 
 
 def gradients(part_ref, live_ref, base_ref, out_ref, square):
     whole = jnp.sum(part_ref[...].astype(f32), 0)
-    whole = jnp.where(live_ref[...] > 0.0, whole, 0.0)
+    turned = pltpu.roll(whole, MINE * SLOTS, 1)
     flat = []
     for q in range(MINE):
-        rows = whole[q * SLOTS : (q + 1) * SLOTS]
         square[q] = lax.dot_general(
-            rows[:, WIDTH:], rows[:, :WIDTH], TN, precision=lax.Precision.HIGHEST, preferred_element_type=f32
+            jnp.where(live_ref[q] > 0.0, turned, 0.0),
+            whole,
+            NT,
+            precision=lax.Precision.HIGHEST,
+            preferred_element_type=f32,
         )
         step = WIDTH // RANKS
         lines = [square[q, pl.ds(r, RANKS, stride=step), :] for r in range(step)]
@@ -193,22 +197,21 @@
 
 
 def local(act_in, grad_out, proj_in, proj_out, lengths, sources, val_feats, val_sets):
-    rows = act_in.shape[0]
     chunks = (HALVES * RANKS, 8, FEATS)
     args = (act_in, grad_out, proj_in.T, proj_out.T, lengths, sources, val_sets.T, val_feats)
     homes = [pltpu.VMEM] * 4 + [pltpu.SMEM] * 3 + [pltpu.VMEM]
     part, live, base, lay = call(
         project,
         [
-            pltpu.VMEM((rows, 2 * WIDTH), bf16),
-            pltpu.VMEM((MINE * SLOTS, 2 * WIDTH), f32),
+            pltpu.VMEM((RANKS, WIDTH, 2 * MINE * SLOTS), bf16),
+            pltpu.VMEM((MINE, WIDTH, 2 * WIDTH), f32),
             pltpu.VMEM(chunks, f32),
             pltpu.VMEM(chunks, f32),
         ],
         [HBM] * 8,
-        [home(x.shape, x.dtype) for home, x in zip(homes, args)] + [pltpu.SemaphoreType.DMA((6 + 2 * PIECES,))],
+        [home(x.shape, x.dtype) for home, x in zip(homes, args)] + [pltpu.SemaphoreType.DMA((6 + len(CUTS),))],
     )(*(far(x) for x in args))
-    part = exchange(part.reshape(RANKS, MINE * SLOTS, 2 * WIDTH), TENSOR)
+    part = exchange(part, TENSOR)
     block = call(gradients, pltpu.VMEM(chunks, bf16), [VMEM] * 3, [pltpu.VMEM((MINE, WIDTH, WIDTH), f32)])(
         here(part), here(live), here(base)
     )

time: 73.5 us -> 73 us (level)
  no operation moved by 1% of the time
where the time goes in v4:
time: 73 us; the launch traced here: 72.8 us
  blocking collectives  67 us (92%)
  Pallas kernels  5.09 us (7%)
    all_to_all x4, blocking collectives, exchange(): return lax.all_to_all(blocks, axes, 0, 0, tiled=True)  67 us
    pallas_call x1, Pallas kernels, local(): call(project, [pltpu.VMEM((RANKS, WIDTH, 2 * MINE * SLOTS), bf16), pltpu....  3.22 us

profile of v4, /device:TPU:1, one launch (start us, length us, event | category | flops | bytes accessed | tf_op | source)
XLA Modules:
  0.0 72.8 jit_solution(4575289765350339820)
XLA Ops:
  0.6 3.2 %shard_map.103 = (bf16[16,64,128]{2,1,0:T(8,128)(2,1)S(1)}, f32[2,64,128]{2,1,0:T(8,128)S(1)}, f32[32,8,256]{2,1,0:T(8,128)S(1)}, f32[32,8,256]{2,1,0:T(8,128)S(1)}) custom-call(bf16[1024,1792]{1,0:T(8,128)(2,1)} %refs_0_.1, bf16[1024,512]{1,0:T(8,128)(2,1)} %refs_1_.1, bf16[64,1792]{1,0:T(8,128)(2,1)} %bitcast.4, bf16[64,512]{1,0:T(8,128)(2,1)} %bitcast.5, ...), custom_call_target="tpu_custom_call" | custom-call | tf_op jit(solution)/shard_map/pallas_call | solution.py:203
  3.9 19.7 %all_to_all.20.part_ref = bf16[16,64,128]{2,1,0:T(8,128)(2,1)S(1)} all-to-all(bf16[16,64,128]{2,1,0:T(8,128)(2,1)S(1)} %get-tuple-element.13), channel_id=1, replica_groups=mesh['y'=8,'h'=2,'c'=2,'z'=4,'x'=4] {'z','x'}, dimensions={0} | all-to-all | bytes 524288 | tf_op jit(solution)/shard_map/all_to_all | solution.py:196
  23.5 0.4 shard_map.104
  24.0 16.9 %all_to_all.21.got_ref = bf16[32,8,256]{2,1,0:T(8,128)(2,1)S(1)} all-to-all(bf16[32,8,256]{2,1,0:T(8,128)(2,1)S(1)} %shard_map.104), channel_id=1, replica_groups=mesh['y'=8,'h'=2,'c'=2,'z'=4,'x'=4] {'h','z','x'}, dimensions={0} | all-to-all | bytes 262144 | tf_op jit(solution)/shard_map/all_to_all | solution.py:196
  40.8 0.3 shard_map.105
  41.1 20.3 %all_to_all.22.came_ref = bf16[16,16,256]{2,1,0:T(8,128)(2,1)S(1)} all-to-all(bf16[16,16,256]{2,1,0:T(8,128)(2,1)S(1)} %shard_map.105), channel_id=1, replica_groups=mesh['y'=8,'h'=2,'c'=2,'z'=4,'x'=4] {'y','c'}, dimensions={0} | all-to-all | bytes 262144 | tf_op jit(solution)/shard_map/all_to_all | solution.py:196
  61.4 0.4 shard_map.106
  61.8 10.2 %all_to_all.23.parts_ref = f32[16,8,128]{2,1,0:T(8,128)S(1)} all-to-all(f32[16,8,128]{2,1,0:T(8,128)S(1)} %get-tuple-element.17), channel_id=1, replica_groups=mesh['y'=8,'h'=2,'c'=2,'z'=4,'x'=4] {'z','x'}, dimensions={0} | all-to-all | bytes 131072 | tf_op jit(solution)/shard_map/all_to_all | solution.py:196
  72.0 0.7 %shard_map.107 = (f32[8,128]{1,0:T(8,128)}, f32[4,8]{1,0:T(4,128)}, f32[8,256]{1,0:T(8,128)}) custom-call(f32[16,8,128]{2,1,0:T(8,128)S(1)} %all_to_all.23.parts_ref, f32[8,128]{1,0:T(8,128)S(1)} %get-tuple-element.18.sets_ref, f32[8,256]{1,0:T(8,128)S(1)} %get-tuple-element.19.grads_ref), custom_call_target="tpu_custom_call" | custom-call | tf_op jit(solution)/shard_map/pallas_call | solution.py:231

commit v5 on v4

--- a/solution.py
+++ b/solution.py
@@ -20,7 +20,9 @@
 NVAL = 128
 CAP = 2
 LOT = HALVES * CAP
+LINE = 3 * FEATS + 128
 NONE = 256.0
+MARK = 136
 CUTS = (0, 256, 512, 1024, 1536, 1792)
 bf16, f32, i32 = jnp.bfloat16, jnp.float32, jnp.int32
 NT = (((1,), (1,)), ((), ()))
@@ -31,15 +33,15 @@
     return lax.broadcasted_iota(i32, shape, dim)
 
 
-def tell(lengths, sources, sets, val, live_ref, base_ref, lay_ref):
-    rank, half, dp = lax.axis_index(TENSOR), lax.axis_index("h"), lax.axis_index(DP)
+def tell(lengths, sources, sets, val, live_ref, base_ref, lay_ref, mark_ref):
+    rank, half = lax.axis_index(TENSOR), lax.axis_index("h")
     for q in range(MINE):
         slot = iota((WIDTH, 2 * WIDTH), 1) - q * SLOTS
         live_ref[q] = jnp.where((slot >= 0) & (slot < lengths[rank * MINE + q]), 1.0, 0.0)
     lane = iota((1, FEATS), 1)
     marks = jnp.zeros((1, FEATS), f32)
     for r in range(VALS):
-        marks = jnp.where(lane == dp * VALS + r, (sets[0, r] + 1).astype(f32), marks)
+        marks = jnp.where(lane == MARK + half * VALS + r, (sets[0, r] + 1).astype(f32), marks)
     told = []
     for q in range(MINE):
         s = rank * MINE + q
@@ -50,10 +52,10 @@
             same = (sources[other] // SRC_DEV == owner) & (other < s)
             order = order + same.astype(i32)
         dest = owner // (HALVES * CORES) * CORES + owner % CORES
-        told.append((owner // CORES % HALVES, dest * 16 + half * CAP + order, source % SRC_DEV + 1))
+        told.append((owner // CORES % HALVES, dest * 8 + half * CAP + order, source % SRC_DEV + 1))
     shape = (RANKS, 8, FEATS)
     row, chunk = iota(shape, 1), iota(shape, 0)
-    over = iota(shape, 2) % 16
+    over, odd = iota(shape, 2) % 8, iota(shape, 2) // 128
     base_ref[0] = jnp.zeros((8, FEATS), f32)
     base_ref[0, 2 : 2 + VALS, :] = val[...].astype(f32)
     rows = jnp.broadcast_to(base_ref[0][None], shape)
@@ -63,17 +65,18 @@
         for q in range(MINE):
             to, slot, tag = told[q]
             slot = jnp.where(to == h, slot, jnp.int32(NONE)).astype(f32)
-            line = jnp.where(lane < 128, slot, tag.astype(f32))
+            line = jnp.where(lane < 128, slot, jnp.where(lane < MARK, tag.astype(f32), 0.0))
             sent = jnp.where(row == 6 + q, jnp.broadcast_to(line[None], shape), sent)
         base_ref[pl.ds(h * RANKS, RANKS)] = sent
-        is_val = (chunk == rank) & (over == LOT + h * VALS + row - 2)
-        is_set = (chunk == (rank + 1) % RANKS) & (row == 2) & (over == LOT + HALVES * VALS)
-        lay = (row >= 2) & (row < 2 + VALS) & (is_val | is_set)
+        which = h * VALS + row - 2
+        lay = (chunk == rank) & (row >= 2) & (row < 2 + VALS) & (which % 2 == odd) & (which // 2 == over)
         lay_ref[pl.ds(h * RANKS, RANKS)] = jnp.where(lay, 1.0, 0.0)
+        lay = (chunk == (rank + 1) % RANKS) & (row == 2) & (over == 0)
+        mark_ref[pl.ds(h * RANKS, RANKS)] = jnp.where(lay, 1.0, 0.0)[:, :, :128]
 
 
 def project(*refs):
-    sources, (part_ref, live_ref, base_ref, lay_ref), held, sems = refs[:8], refs[8:12], refs[12:20], refs[20]
+    sources, (part_ref, *told), held, sems = refs[:8], refs[8:13], refs[13:21], refs[21]
     act, grad, pin, pout, lengths, owners, sets, val = held
     moves = [(sources[i], held[i]) for i in (4, 5, 6, 7, 3, 1, 2)]
     cuts = [pl.ds(lo, hi - lo) for lo, hi in zip(CUTS[:-1], CUTS[1:])]
@@ -83,7 +86,7 @@
         copy.start()
     for copy in copies[:4]:
         copy.wait()
-    tell(lengths, owners, sets, val, live_ref, base_ref, lay_ref)
+    tell(lengths, owners, sets, val, *told)
     copies[4].wait()
     copies[5].wait()
     out = lax.dot_general(pout[...], grad[...], NT, preferred_element_type=f32)
@@ -124,36 +127,45 @@
         out_ref[cut] = sent.astype(bf16)
 
 
-def pack(got_ref, lay_ref, out_ref):
+def pack(got_ref, lay_ref, mark_ref, out_ref):
     x = got_ref[...].astype(f32)
-    row, lane = iota(x.shape, 1), iota(x.shape, 2)
-    turned = pltpu.roll(x, 2, 1)
-    slot = jnp.concatenate([turned[:, :, :128]] * 2, 2).astype(i32)
-    told = jnp.concatenate([x[:, :, :128]] * 2, 2).astype(i32)
-    moves = ((row < 2) & (slot == lane)) | ((row >= 6) & (told + LOT + HALVES * VALS == lane))
-    moves = jnp.where(moves, 1.0, lay_ref[...]).reshape(-1, FEATS).astype(bf16)
-    x = jnp.where((row >= 6) & (lane < 128), 0.0, x).reshape(-1, FEATS).astype(bf16)
-    packed = lax.dot_general(moves, x, TN, preferred_element_type=f32)
-    out_ref[...] = packed.astype(bf16).reshape(out_ref.shape)
+    told = x[:, :, :128].astype(i32)
+    slot = pltpu.roll(x[:, :, :128], 2, 1).astype(i32)
+    row, lane = iota(told.shape, 1), iota(told.shape, 2)
+    grads = jnp.where((row < 2) & (slot == lane), 1.0, 0.0)
+    marks = jnp.where((row >= 6) & (told == lane), 1.0, mark_ref[...])
+    moves = jnp.concatenate([grads, lay_ref[...], marks], 2).reshape(-1, 512).astype(bf16)
+    x = x.reshape(-1, FEATS).astype(bf16)
+    packed = lax.dot_general(moves[:, :384], x, TN, preferred_element_type=f32)
+    small = lax.dot_general(moves[:, 384:], x[:, 128:], TN, preferred_element_type=f32)
+    pieces = [packed[k * 128 : (k + 1) * 128].reshape(DESTS, 8, FEATS) for k in range(3)]
+    pieces.append(small.reshape(DESTS, 8, 128))
+    out_ref[...] = jnp.concatenate(pieces, 2)[:, :LOT].astype(bf16)
 
 
 def score(came_ref, grads_ref, spread_ref, sets_ref):
-    x = came_ref[...].astype(f32).reshape(-1, FEATS)
-    rows = x.shape[0]
-    half = x[:, :128]
-    row = iota(half.shape, 0) % 16
-    tags = pltpu.roll(x, rows - (LOT + HALVES * VALS), 0)[:, 128:].astype(i32)
-    chooser = jnp.where((row < LOT) & (tags == iota(half.shape, 1) + 1), 1.0, 0.0).astype(bf16)
+    x = came_ref[...].astype(f32)
+    x = jnp.concatenate([x, jnp.zeros(x.shape, f32)], 1).reshape(DESTS * 8, LINE)
+    small = x[:, 3 * FEATS :]
+    n, lane = iota(small.shape, 0), iota(small.shape, 1)
+    chooser = jnp.where(small.astype(i32) == lane + 1, 1.0, 0.0).astype(bf16)
     x = x.astype(bf16)
-    source_grads = lax.dot_general(chooser, x, TN, preferred_element_type=f32)[:SRC_DEV]
+    source_grads = lax.dot_general(chooser, x[:, :FEATS], TN, preferred_element_type=f32)[:SRC_DEV]
     grads_ref[...] = source_grads
-    sets_ref[...] = jnp.broadcast_to(
-        jnp.sum(jnp.where(row == LOT + HALVES * VALS, half, 0.0), 0, keepdims=True), sets_ref.shape
-    )
-    v, n = iota((NVAL, rows), 0), iota((NVAL, rows), 1)
-    r, c, h, y = v % VALS, v // VALS % CORES, v // (VALS * CORES) % HALVES, v // (VALS * CORES * HALVES)
-    pick = n == (y * CORES + c) * 16 + LOT + h * VALS + r
-    val = jnp.dot(jnp.where(pick, 1.0, 0.0).astype(bf16), x, preferred_element_type=f32)
+
+    def parts(v):
+        return v % VALS, v // VALS % CORES, v // (VALS * CORES) % HALVES, v // (VALS * CORES * HALVES)
+
+    r, c, h, y = parts(lane)
+    spread = jnp.where(n == MARK - 128 + h * VALS + r, 1.0, 0.0).astype(bf16)
+    marks = jnp.dot(small.astype(bf16), spread, preferred_element_type=f32)
+    marks = jnp.sum(jnp.where(n == (y * CORES + c) * 8, marks, 0.0), 0, keepdims=True)
+    sets_ref[...] = jnp.broadcast_to(marks, sets_ref.shape)
+    shape = (NVAL, 2 * DESTS * 8)
+    r, c, h, y = parts(iota(shape, 0))
+    pick = iota(shape, 1) == r % 2 * (DESTS * 8) + (y * CORES + c) * 8 + (h * VALS + r) // 2
+    val = jnp.concatenate([x[:, FEATS : 2 * FEATS], x[:, 2 * FEATS : 3 * FEATS]], 0)
+    val = jnp.dot(jnp.where(pick, 1.0, 0.0).astype(bf16), val, preferred_element_type=f32)
     pair = lax.dot_general(source_grads, val, NT, precision=lax.Precision.HIGHEST, preferred_element_type=f32)
     spread_ref[...] = jnp.broadcast_to(pair[None], spread_ref.shape)
 
@@ -200,13 +212,14 @@
     chunks = (HALVES * RANKS, 8, FEATS)
     args = (act_in, grad_out, proj_in.T, proj_out.T, lengths, sources, val_sets.T, val_feats)
     homes = [pltpu.VMEM] * 4 + [pltpu.SMEM] * 3 + [pltpu.VMEM]
-    part, live, base, lay = call(
+    part, live, base, lay, mark = call(
         project,
         [
             pltpu.VMEM((RANKS, WIDTH, 2 * MINE * SLOTS), bf16),
             pltpu.VMEM((MINE, WIDTH, 2 * WIDTH), f32),
             pltpu.VMEM(chunks, f32),
             pltpu.VMEM(chunks, f32),
+            pltpu.VMEM(chunks[:2] + (128,), f32),
         ],
         [HBM] * 8,
         [home(x.shape, x.dtype) for home, x in zip(homes, args)] + [pltpu.SemaphoreType.DMA((6 + len(CUTS),))],
@@ -216,7 +229,7 @@
         here(part), here(live), here(base)
     )
     got = exchange(block, ("h",) + TENSOR)
-    packed = call(pack, pltpu.VMEM((DESTS, 16, FEATS), bf16), [VMEM] * 2)(here(got), here(lay))
+    packed = call(pack, pltpu.VMEM((DESTS, LOT, LINE), bf16), [VMEM] * 3)(here(got), here(lay), here(mark))
     came = exchange(packed, ("y", "c"))
     source_grads, spread, sets = call(
         score,

time: 73 us -> 72.6 us (level)
  no operation moved by 1% of the time
where the time goes in v5:
time: 72.6 us; the launch traced here: 72.3 us
  blocking collectives  66.6 us (92%)
  Pallas kernels  5.06 us (7%)
    all_to_all x4, blocking collectives, exchange(): return lax.all_to_all(blocks, axes, 0, 0, tiled=True)  66.6 us
    pallas_call x1, Pallas kernels, local(): call(project, [pltpu.VMEM((RANKS, WIDTH, 2 * MINE * SLOTS), bf16), pltpu....  3.22 us

profile of v5, /device:TPU:1, one launch (start us, length us, event | category | flops | bytes accessed | tf_op | source)
XLA Modules:
  0.0 72.3 jit_solution(16270911655880685803)
XLA Ops:
  0.6 3.2 %shard_map.103 = (bf16[16,64,128]{2,1,0:T(8,128)(2,1)S(1)}, f32[2,64,128]{2,1,0:T(8,128)S(1)}, f32[32,8,256]{2,1,0:T(8,128)S(1)}, f32[32,8,256]{2,1,0:T(8,128)S(1)}, f32[32,8,128]{2,1,0:T(8,128)S(1)}) custom-call(bf16[1024,1792]{1,0:T(8,128)(2,1)} %refs_0_.1, bf16[1024,512]{1,0:T(8,128)(2,1)} %refs_1_.1, bf16[64,1792]{1,0:T(8,128)(2,1)} %bitcast.4, ...), custom_call_target="tpu_custom_call" | custom-call | tf_op jit(solution)/shard_map/pallas_call | solution.py:215
  3.9 19.7 %all_to_all.20.part_ref = bf16[16,64,128]{2,1,0:T(8,128)(2,1)S(1)} all-to-all(bf16[16,64,128]{2,1,0:T(8,128)(2,1)S(1)} %get-tuple-element.14), channel_id=1, replica_groups=mesh['y'=8,'h'=2,'c'=2,'z'=4,'x'=4] {'z','x'}, dimensions={0} | all-to-all | bytes 524288 | tf_op jit(solution)/shard_map/all_to_all | solution.py:208
  23.5 0.4 shard_map.104
  24.0 16.9 %all_to_all.21.got_ref = bf16[32,8,256]{2,1,0:T(8,128)(2,1)S(1)} all-to-all(bf16[32,8,256]{2,1,0:T(8,128)(2,1)S(1)} %shard_map.104), channel_id=1, replica_groups=mesh['y'=8,'h'=2,'c'=2,'z'=4,'x'=4] {'h','z','x'}, dimensions={0} | all-to-all | bytes 262144 | tf_op jit(solution)/shard_map/all_to_all | solution.py:208
  40.8 0.3 shard_map.105
  41.1 20.0 %all_to_all.22.came_ref = bf16[16,4,896]{2,1,0:T(4,128)(2,1)S(1)} all-to-all(bf16[16,4,896]{2,1,0:T(4,128)(2,1)S(1)} %shard_map.105), channel_id=1, replica_groups=mesh['y'=8,'h'=2,'c'=2,'z'=4,'x'=4] {'y','c'}, dimensions={0} | all-to-all | bytes 229376 | tf_op jit(solution)/shard_map/all_to_all | solution.py:208
  61.1 0.4 shard_map.106
  61.5 10.1 %all_to_all.23.parts_ref = f32[16,8,128]{2,1,0:T(8,128)S(1)} all-to-all(f32[16,8,128]{2,1,0:T(8,128)S(1)} %get-tuple-element.19), channel_id=1, replica_groups=mesh['y'=8,'h'=2,'c'=2,'z'=4,'x'=4] {'z','x'}, dimensions={0} | all-to-all | bytes 131072 | tf_op jit(solution)/shard_map/all_to_all | solution.py:208
  71.6 0.7 %shard_map.107 = (f32[8,128]{1,0:T(8,128)}, f32[4,8]{1,0:T(4,128)}, f32[8,256]{1,0:T(8,128)}) custom-call(f32[16,8,128]{2,1,0:T(8,128)S(1)} %all_to_all.23.parts_ref, f32[8,128]{1,0:T(8,128)S(1)} %get-tuple-element.20.sets_ref, f32[8,256]{1,0:T(8,128)S(1)} %get-tuple-element.21.grads_ref), custom_call_target="tpu_custom_call" | custom-call | tf_op jit(solution)/shard_map/pallas_call | solution.py:244

commit v6 on v5

--- a/solution.py
+++ b/solution.py
@@ -21,8 +21,10 @@
 CAP = 2
 LOT = HALVES * CAP
 LINE = 3 * FEATS + 128
+REST = LINE - FEATS
+MARK = 8
+SLOT = 2 * FEATS + 64
 NONE = 256.0
-MARK = 136
 CUTS = (0, 256, 512, 1024, 1536, 1792)
 bf16, f32, i32 = jnp.bfloat16, jnp.float32, jnp.int32
 NT = (((1,), (1,)), ((), ()))
@@ -38,8 +40,8 @@
     for q in range(MINE):
         slot = iota((WIDTH, 2 * WIDTH), 1) - q * SLOTS
         live_ref[q] = jnp.where((slot >= 0) & (slot < lengths[rank * MINE + q]), 1.0, 0.0)
-    lane = iota((1, FEATS), 1)
-    marks = jnp.zeros((1, FEATS), f32)
+    lane = iota((1, REST), 1)
+    marks = jnp.zeros((1, REST), f32)
     for r in range(VALS):
         marks = jnp.where(lane == MARK + half * VALS + r, (sets[0, r] + 1).astype(f32), marks)
     told = []
@@ -53,26 +55,29 @@
             order = order + same.astype(i32)
         dest = owner // (HALVES * CORES) * CORES + owner % CORES
         told.append((owner // CORES % HALVES, dest * 8 + half * CAP + order, source % SRC_DEV + 1))
-    shape = (RANKS, 8, FEATS)
+    shape = (RANKS, 8, REST)
     row, chunk = iota(shape, 1), iota(shape, 0)
-    over, odd = iota(shape, 2) % 8, iota(shape, 2) // 128
-    base_ref[0] = jnp.zeros((8, FEATS), f32)
-    base_ref[0, 2 : 2 + VALS, :] = val[...].astype(f32)
+    base_ref[0] = jnp.zeros((8, REST), f32)
+    rows = val[...].astype(f32)
+    for r in range(VALS):
+        base_ref[0, r // 2 : r // 2 + 1, r % 2 * FEATS : (r % 2 + 1) * FEATS] = rows[r : r + 1]
     rows = jnp.broadcast_to(base_ref[0][None], shape)
-    rows = jnp.where(chunk == rank, rows, jnp.where(row == 2, jnp.broadcast_to(marks[None], shape), 0.0))
+    rows = jnp.where(chunk == rank, rows, jnp.where(row == 0, jnp.broadcast_to(marks[None], shape), 0.0))
+    small = (RANKS, 8, 128)
+    line, over, owner = iota(small, 1), iota(small, 2) % 8, iota(small, 0)
     for h in range(HALVES):
+        cut = pl.ds(h * RANKS, RANKS)
         sent = rows
         for q in range(MINE):
             to, slot, tag = told[q]
             slot = jnp.where(to == h, slot, jnp.int32(NONE)).astype(f32)
-            line = jnp.where(lane < 128, slot, jnp.where(lane < MARK, tag.astype(f32), 0.0))
-            sent = jnp.where(row == 6 + q, jnp.broadcast_to(line[None], shape), sent)
-        base_ref[pl.ds(h * RANKS, RANKS)] = sent
-        which = h * VALS + row - 2
-        lay = (chunk == rank) & (row >= 2) & (row < 2 + VALS) & (which % 2 == odd) & (which // 2 == over)
-        lay_ref[pl.ds(h * RANKS, RANKS)] = jnp.where(lay, 1.0, 0.0)
-        lay = (chunk == (rank + 1) % RANKS) & (row == 2) & (over == 0)
-        mark_ref[pl.ds(h * RANKS, RANKS)] = jnp.where(lay, 1.0, 0.0)[:, :, :128]
+            word = jnp.where(lane >= SLOT, slot, jnp.where(lane < 2 * FEATS + MARK, tag.astype(f32), 0.0))
+            sent = jnp.where((row == q) & (iota(shape, 2) >= 2 * FEATS), jnp.broadcast_to(word[None], shape), sent)
+        base_ref[cut] = sent
+        lay = (owner == rank) & (line < MINE) & (over == h * MINE + line)
+        lay_ref[cut] = jnp.where(lay, 1.0, 0.0)
+        lay = (owner == (rank + 1) % RANKS) & (line == 0) & (over == 0)
+        mark_ref[cut] = jnp.where(lay, 1.0, 0.0)
 
 
 def project(*refs):
@@ -118,29 +123,27 @@
         lines = [square[q, pl.ds(r, RANKS, stride=step), :] for r in range(step)]
         flat.append(jnp.concatenate(lines, 1))
     shape = (RANKS, 8, FEATS)
-    row = iota(shape, 1)
+    flat = [jnp.broadcast_to(line[:, None, :], shape) for line in flat]
+    flat = jnp.where(iota(shape, 1) == 0, flat[0], flat[1])
     for h in range(HALVES):
         cut = pl.ds(h * RANKS, RANKS)
-        sent = base_ref[cut]
-        for q in range(MINE):
-            sent = jnp.where(row == q, jnp.broadcast_to(flat[q][:, None, :], shape), sent)
-        out_ref[cut] = sent.astype(bf16)
+        out_ref[cut] = jnp.concatenate([flat, base_ref[cut]], 2)[:, :MINE].astype(bf16)
 
 
 def pack(got_ref, lay_ref, mark_ref, out_ref):
     x = got_ref[...].astype(f32)
-    told = x[:, :, :128].astype(i32)
-    slot = pltpu.roll(x[:, :, :128], 2, 1).astype(i32)
-    row, lane = iota(told.shape, 1), iota(told.shape, 2)
-    grads = jnp.where((row < 2) & (slot == lane), 1.0, 0.0)
-    marks = jnp.where((row >= 6) & (told == lane), 1.0, mark_ref[...])
-    moves = jnp.concatenate([grads, lay_ref[...], marks], 2).reshape(-1, 512).astype(bf16)
-    x = x.reshape(-1, FEATS).astype(bf16)
-    packed = lax.dot_general(moves[:, :384], x, TN, preferred_element_type=f32)
-    small = lax.dot_general(moves[:, 384:], x[:, 128:], TN, preferred_element_type=f32)
-    pieces = [packed[k * 128 : (k + 1) * 128].reshape(DESTS, 8, FEATS) for k in range(3)]
-    pieces.append(small.reshape(DESTS, 8, 128))
-    out_ref[...] = jnp.concatenate(pieces, 2)[:, :LOT].astype(bf16)
+    x = jnp.concatenate([x, jnp.zeros((x.shape[0], 8 - MINE, LINE), f32)], 1)
+    shape = x.shape[:2] + (128,)
+    slot = jnp.broadcast_to(x[:, :, FEATS + SLOT : FEATS + SLOT + 1], shape).astype(i32)
+    moves = jnp.where((iota(shape, 1) < MINE) & (slot == iota(shape, 2)), 1.0, 0.0)
+    moves, lay, mark = (m.reshape(-1, 128).astype(bf16) for m in (moves, lay_ref[...], mark_ref[...]))
+    x = x.reshape(-1, LINE).astype(bf16)
+    own = jnp.concatenate([x[:, :FEATS], x[:, 3 * FEATS :]], 1)
+    own = lax.dot_general(moves, own, TN, preferred_element_type=f32)
+    val = lax.dot_general(lay, x[:, FEATS : 3 * FEATS], TN, preferred_element_type=f32)
+    marks = lax.dot_general(mark, x[:, FEATS : FEATS + 128], TN, preferred_element_type=f32)
+    out = jnp.concatenate([own[:, :FEATS], val, own[:, FEATS:] + marks], 1)
+    out_ref[...] = out.reshape(DESTS, 8, LINE)[:, :LOT].astype(bf16)
 
 
 def score(came_ref, grads_ref, spread_ref, sets_ref):
@@ -157,7 +160,7 @@
         return v % VALS, v // VALS % CORES, v // (VALS * CORES) % HALVES, v // (VALS * CORES * HALVES)
 
     r, c, h, y = parts(lane)
-    spread = jnp.where(n == MARK - 128 + h * VALS + r, 1.0, 0.0).astype(bf16)
+    spread = jnp.where(n == MARK + h * VALS + r, 1.0, 0.0).astype(bf16)
     marks = jnp.dot(small.astype(bf16), spread, preferred_element_type=f32)
     marks = jnp.sum(jnp.where(n == (y * CORES + c) * 8, marks, 0.0), 0, keepdims=True)
     sets_ref[...] = jnp.broadcast_to(marks, sets_ref.shape)
@@ -209,7 +212,7 @@
 
 
 def local(act_in, grad_out, proj_in, proj_out, lengths, sources, val_feats, val_sets):
-    chunks = (HALVES * RANKS, 8, FEATS)
+    chunks = HALVES * RANKS
     args = (act_in, grad_out, proj_in.T, proj_out.T, lengths, sources, val_sets.T, val_feats)
     homes = [pltpu.VMEM] * 4 + [pltpu.SMEM] * 3 + [pltpu.VMEM]
     part, live, base, lay, mark = call(
@@ -217,15 +220,15 @@
         [
             pltpu.VMEM((RANKS, WIDTH, 2 * MINE * SLOTS), bf16),
             pltpu.VMEM((MINE, WIDTH, 2 * WIDTH), f32),
-            pltpu.VMEM(chunks, f32),
-            pltpu.VMEM(chunks, f32),
-            pltpu.VMEM(chunks[:2] + (128,), f32),
+            pltpu.VMEM((chunks, 8, REST), f32),
+            pltpu.VMEM((chunks, 8, 128), f32),
+            pltpu.VMEM((chunks, 8, 128), f32),
         ],
         [HBM] * 8,
         [home(x.shape, x.dtype) for home, x in zip(homes, args)] + [pltpu.SemaphoreType.DMA((6 + len(CUTS),))],
     )(*(far(x) for x in args))
     part = exchange(part, TENSOR)
-    block = call(gradients, pltpu.VMEM(chunks, bf16), [VMEM] * 3, [pltpu.VMEM((MINE, WIDTH, WIDTH), f32)])(
+    block = call(gradients, pltpu.VMEM((chunks, MINE, LINE), bf16), [VMEM] * 3, [pltpu.VMEM((MINE, WIDTH, WIDTH), f32)])(
         here(part), here(live), here(base)
     )
     got = exchange(block, ("h",) + TENSOR)

time: 72.6 us -> 72.5 us (level)
  no operation moved by 1% of the time
where the time goes in v6:
time: 72.5 us; the launch traced here: 72.3 us
  blocking collectives  66.5 us (92%)
  Pallas kernels  5.16 us (7%)
    all_to_all x4, blocking collectives, exchange(): return lax.all_to_all(blocks, axes, 0, 0, tiled=True)  66.5 us
    pallas_call x1, Pallas kernels, local(): call(project, [pltpu.VMEM((RANKS, WIDTH, 2 * MINE * SLOTS), bf16), pltpu....  3.22 us

profile of v6, /device:TPU:1, one launch (start us, length us, event | category | flops | bytes accessed | tf_op | source)
XLA Modules:
  0.0 72.3 jit_solution(12245619199176285137)
XLA Ops:
  0.6 3.2 %shard_map.103 = (bf16[16,64,128]{2,1,0:T(8,128)(2,1)S(1)}, f32[2,64,128]{2,1,0:T(8,128)S(1)}, f32[32,8,640]{2,1,0:T(8,128)S(1)}, f32[32,8,128]{2,1,0:T(8,128)S(1)}, f32[32,8,128]{2,1,0:T(8,128)S(1)}) custom-call(bf16[1024,1792]{1,0:T(8,128)(2,1)} %refs_0_.1, bf16[1024,512]{1,0:T(8,128)(2,1)} %refs_1_.1, bf16[64,1792]{1,0:T(8,128)(2,1)} %bitcast.4, ...), custom_call_target="tpu_custom_call" | custom-call | tf_op jit(solution)/shard_map/pallas_call | solution.py:218
  3.9 19.7 %all_to_all.20.part_ref = bf16[16,64,128]{2,1,0:T(8,128)(2,1)S(1)} all-to-all(bf16[16,64,128]{2,1,0:T(8,128)(2,1)S(1)} %get-tuple-element.14), channel_id=1, replica_groups=mesh['y'=8,'h'=2,'c'=2,'z'=4,'x'=4] {'z','x'}, dimensions={0} | all-to-all | bytes 524288 | tf_op jit(solution)/shard_map/all_to_all | solution.py:211
  23.5 0.4 shard_map.104
  24.0 16.7 %all_to_all.21.got_ref = bf16[32,2,896]{2,1,0:T(2,128)(2,1)S(1)} all-to-all(bf16[32,2,896]{2,1,0:T(2,128)(2,1)S(1)} %shard_map.104), channel_id=1, replica_groups=mesh['y'=8,'h'=2,'c'=2,'z'=4,'x'=4] {'h','z','x'}, dimensions={0} | all-to-all | bytes 229376 | tf_op jit(solution)/shard_map/all_to_all | solution.py:211
  40.7 0.4 shard_map.105
  41.1 20.0 %all_to_all.22.came_ref = bf16[16,4,896]{2,1,0:T(4,128)(2,1)S(1)} all-to-all(bf16[16,4,896]{2,1,0:T(4,128)(2,1)S(1)} %shard_map.105), channel_id=1, replica_groups=mesh['y'=8,'h'=2,'c'=2,'z'=4,'x'=4] {'y','c'}, dimensions={0} | all-to-all | bytes 229376 | tf_op jit(solution)/shard_map/all_to_all | solution.py:211
  61.0 0.4 shard_map.106
  61.4 10.1 %all_to_all.23.parts_ref = f32[16,8,128]{2,1,0:T(8,128)S(1)} all-to-all(f32[16,8,128]{2,1,0:T(8,128)S(1)} %get-tuple-element.19), channel_id=1, replica_groups=mesh['y'=8,'h'=2,'c'=2,'z'=4,'x'=4] {'z','x'}, dimensions={0} | all-to-all | bytes 131072 | tf_op jit(solution)/shard_map/all_to_all | solution.py:211
  71.5 0.7 %shard_map.107 = (f32[8,128]{1,0:T(8,128)}, f32[4,8]{1,0:T(4,128)}, f32[8,256]{1,0:T(8,128)}) custom-call(f32[16,8,128]{2,1,0:T(8,128)S(1)} %all_to_all.23.parts_ref, f32[8,128]{1,0:T(8,128)S(1)} %get-tuple-element.20.sets_ref, f32[8,256]{1,0:T(8,128)S(1)} %get-tuple-element.21.grads_ref), custom_call_target="tpu_custom_call" | custom-call | tf_op jit(solution)/shard_map/pallas_call | solution.py:247

commit v7 on v6

--- a/solution.py
+++ b/solution.py
@@ -35,11 +35,26 @@
     return lax.broadcasted_iota(i32, shape, dim)
 
 
+def parts(v):
+    return v % VALS, v // VALS % CORES, v // (VALS * CORES) % HALVES, v // (VALS * CORES * HALVES)
+
+
+def fix(fixed_ref):
+    shape = (NVAL, 2 * DESTS * 8)
+    r, c, h, y = parts(iota(shape, 0))
+    pick = iota(shape, 1) == r % 2 * (DESTS * 8) + (y * CORES + c) * 8 + (h * VALS + r) // 2
+    fixed_ref[:, :256] = jnp.where(pick, 1.0, 0.0).astype(bf16)
+    n, v = iota((128, NVAL), 0), iota((128, NVAL), 1)
+    r, c, h, y = parts(v)
+    fixed_ref[:, 256:384] = jnp.where(n == MARK + h * VALS + r, 1.0, 0.0).astype(bf16)
+    fixed_ref[:, 384:] = jnp.where(n == (y * CORES + c) * 8, 1.0, 0.0).astype(bf16)
+
+
 def tell(lengths, sources, sets, val, live_ref, base_ref, lay_ref, mark_ref):
     rank, half = lax.axis_index(TENSOR), lax.axis_index("h")
     for q in range(MINE):
         slot = iota((WIDTH, 2 * WIDTH), 1) - q * SLOTS
-        live_ref[q] = jnp.where((slot >= 0) & (slot < lengths[rank * MINE + q]), 1.0, 0.0)
+        live_ref[q * WIDTH : (q + 1) * WIDTH, :] = jnp.where((slot >= 0) & (slot < lengths[rank * MINE + q]), 1.0, 0.0)
     lane = iota((1, REST), 1)
     marks = jnp.zeros((1, REST), f32)
     for r in range(VALS):
@@ -81,7 +96,7 @@
 
 
 def project(*refs):
-    sources, (part_ref, *told), held, sems = refs[:8], refs[8:13], refs[13:21], refs[21]
+    sources, (part_ref, fixed_ref, *told), held, sems = refs[:8], refs[8:14], refs[14:22], refs[22]
     act, grad, pin, pout, lengths, owners, sets, val = held
     moves = [(sources[i], held[i]) for i in (4, 5, 6, 7, 3, 1, 2)]
     cuts = [pl.ds(lo, hi - lo) for lo, hi in zip(CUTS[:-1], CUTS[1:])]
@@ -89,6 +104,7 @@
     copies = [pltpu.make_async_copy(*move, sems.at[i]) for i, move in enumerate(moves)]
     for copy in copies:
         copy.start()
+    fix(fixed_ref)
     for copy in copies[:4]:
         copy.wait()
     tell(lengths, owners, sets, val, *told)
@@ -110,17 +126,14 @@
 def gradients(part_ref, live_ref, base_ref, out_ref, square):
     whole = jnp.sum(part_ref[...].astype(f32), 0)
     turned = pltpu.roll(whole, MINE * SLOTS, 1)
+    turned = jnp.where(live_ref[...] > 0.0, jnp.concatenate([turned] * MINE, 0), 0.0)
+    square[...] = lax.dot_general(
+        turned, whole, NT, precision=lax.Precision.HIGHEST, preferred_element_type=f32
+    )
+    step = WIDTH // RANKS
     flat = []
     for q in range(MINE):
-        square[q] = lax.dot_general(
-            jnp.where(live_ref[q] > 0.0, turned, 0.0),
-            whole,
-            NT,
-            precision=lax.Precision.HIGHEST,
-            preferred_element_type=f32,
-        )
-        step = WIDTH // RANKS
-        lines = [square[q, pl.ds(r, RANKS, stride=step), :] for r in range(step)]
+        lines = [square[pl.ds(q * WIDTH + r, RANKS, stride=step), :] for r in range(step)]
         flat.append(jnp.concatenate(lines, 1))
     shape = (RANKS, 8, FEATS)
     flat = [jnp.broadcast_to(line[:, None, :], shape) for line in flat]
@@ -146,29 +159,20 @@
     out_ref[...] = out.reshape(DESTS, 8, LINE)[:, :LOT].astype(bf16)
 
 
-def score(came_ref, grads_ref, spread_ref, sets_ref):
+def score(came_ref, fixed_ref, grads_ref, spread_ref, sets_ref):
     x = came_ref[...].astype(f32)
     x = jnp.concatenate([x, jnp.zeros(x.shape, f32)], 1).reshape(DESTS * 8, LINE)
     small = x[:, 3 * FEATS :]
-    n, lane = iota(small.shape, 0), iota(small.shape, 1)
+    lane = iota(small.shape, 1)
     chooser = jnp.where(small.astype(i32) == lane + 1, 1.0, 0.0).astype(bf16)
     x = x.astype(bf16)
     source_grads = lax.dot_general(chooser, x[:, :FEATS], TN, preferred_element_type=f32)[:SRC_DEV]
     grads_ref[...] = source_grads
-
-    def parts(v):
-        return v % VALS, v // VALS % CORES, v // (VALS * CORES) % HALVES, v // (VALS * CORES * HALVES)
-
-    r, c, h, y = parts(lane)
-    spread = jnp.where(n == MARK + h * VALS + r, 1.0, 0.0).astype(bf16)
-    marks = jnp.dot(small.astype(bf16), spread, preferred_element_type=f32)
-    marks = jnp.sum(jnp.where(n == (y * CORES + c) * 8, marks, 0.0), 0, keepdims=True)
+    marks = jnp.dot(small.astype(bf16), fixed_ref[:, 256:384], preferred_element_type=f32)
+    marks = jnp.sum(marks * fixed_ref[:, 384:].astype(f32), 0, keepdims=True)
     sets_ref[...] = jnp.broadcast_to(marks, sets_ref.shape)
-    shape = (NVAL, 2 * DESTS * 8)
-    r, c, h, y = parts(iota(shape, 0))
-    pick = iota(shape, 1) == r % 2 * (DESTS * 8) + (y * CORES + c) * 8 + (h * VALS + r) // 2
     val = jnp.concatenate([x[:, FEATS : 2 * FEATS], x[:, 2 * FEATS : 3 * FEATS]], 0)
-    val = jnp.dot(jnp.where(pick, 1.0, 0.0).astype(bf16), val, preferred_element_type=f32)
+    val = jnp.dot(fixed_ref[:, :256], val, preferred_element_type=f32)
     pair = lax.dot_general(source_grads, val, NT, precision=lax.Precision.HIGHEST, preferred_element_type=f32)
     spread_ref[...] = jnp.broadcast_to(pair[None], spread_ref.shape)
 
@@ -215,11 +219,12 @@
     chunks = HALVES * RANKS
     args = (act_in, grad_out, proj_in.T, proj_out.T, lengths, sources, val_sets.T, val_feats)
     homes = [pltpu.VMEM] * 4 + [pltpu.SMEM] * 3 + [pltpu.VMEM]
-    part, live, base, lay, mark = call(
+    part, fixed, live, base, lay, mark = call(
         project,
         [
             pltpu.VMEM((RANKS, WIDTH, 2 * MINE * SLOTS), bf16),
-            pltpu.VMEM((MINE, WIDTH, 2 * WIDTH), f32),
+            pltpu.VMEM((NVAL, 512), bf16),
+            pltpu.VMEM((MINE * WIDTH, 2 * WIDTH), f32),
             pltpu.VMEM((chunks, 8, REST), f32),
             pltpu.VMEM((chunks, 8, 128), f32),
             pltpu.VMEM((chunks, 8, 128), f32),
@@ -228,7 +233,7 @@
         [home(x.shape, x.dtype) for home, x in zip(homes, args)] + [pltpu.SemaphoreType.DMA((6 + len(CUTS),))],
     )(*(far(x) for x in args))
     part = exchange(part, TENSOR)
-    block = call(gradients, pltpu.VMEM((chunks, MINE, LINE), bf16), [VMEM] * 3, [pltpu.VMEM((MINE, WIDTH, WIDTH), f32)])(
+    block = call(gradients, pltpu.VMEM((chunks, MINE, LINE), bf16), [VMEM] * 3, [pltpu.VMEM((MINE * WIDTH, WIDTH), f32)])(
         here(part), here(live), here(base)
     )
     got = exchange(block, ("h",) + TENSOR)
@@ -241,8 +246,8 @@
             pltpu.VMEM((RANKS, SRC_DEV, NVAL), f32),
             pltpu.VMEM((8, NVAL), f32),
         ],
-        [VMEM],
-    )(here(came))
+        [VMEM] * 2,
+    )(here(came), here(fixed))
     parts = exchange(spread, TENSOR)
     pair_scores, set_scores, source_grads = call(
         finish,

time: 72.5 us -> 72.5 us (level)
  no operation moved by 1% of the time
where the time goes in v7:
time: 72.5 us; the launch traced here: 72.3 us
  blocking collectives  66.5 us (92%)
  Pallas kernels  5.14 us (7%)
    all_to_all x4, blocking collectives, exchange(): return lax.all_to_all(blocks, axes, 0, 0, tiled=True)  66.5 us
    pallas_call x1, Pallas kernels, local(): call(project, [pltpu.VMEM((RANKS, WIDTH, 2 * MINE * SLOTS), bf16), pltpu....  3.22 us

profile of v7, /device:TPU:1, one launch (start us, length us, event | category | flops | bytes accessed | tf_op | source)
XLA Modules:
  0.0 72.3 jit_solution(11944254542952105012)
XLA Ops:
  0.6 3.2 %shard_map.103 = (bf16[16,64,128]{2,1,0:T(8,128)(2,1)S(1)}, bf16[128,512]{1,0:T(8,128)(2,1)S(1)}, f32[128,128]{1,0:T(8,128)S(1)}, f32[32,8,640]{2,1,0:T(8,128)S(...) custom-call(bf16[1024,1792]{1,0:T(8,128)(2,1)} %refs_0_.1, bf16[1024,512]{1,0:T(8,128)(2,1)} %refs_1_.1, ...), custom_call_target="tpu_custom_call" | custom-call | tf_op jit(solution)/shard_map/pallas_call | solution.py:222
  3.9 19.7 %all_to_all.20.part_ref = bf16[16,64,128]{2,1,0:T(8,128)(2,1)S(1)} all-to-all(bf16[16,64,128]{2,1,0:T(8,128)(2,1)S(1)} %get-tuple-element.15), channel_id=1, replica_groups=mesh['y'=8,'h'=2,'c'=2,'z'=4,'x'=4] {'z','x'}, dimensions={0} | all-to-all | bytes 524288 | tf_op jit(solution)/shard_map/all_to_all | solution.py:215
  23.5 0.4 shard_map.104
  23.9 16.7 %all_to_all.21.got_ref = bf16[32,2,896]{2,1,0:T(2,128)(2,1)S(1)} all-to-all(bf16[32,2,896]{2,1,0:T(2,128)(2,1)S(1)} %shard_map.104), channel_id=1, replica_groups=mesh['y'=8,'h'=2,'c'=2,'z'=4,'x'=4] {'h','z','x'}, dimensions={0} | all-to-all | bytes 229376 | tf_op jit(solution)/shard_map/all_to_all | solution.py:215
  40.7 0.4 shard_map.105
  41.0 20.0 %all_to_all.22.came_ref = bf16[16,4,896]{2,1,0:T(4,128)(2,1)S(1)} all-to-all(bf16[16,4,896]{2,1,0:T(4,128)(2,1)S(1)} %shard_map.105), channel_id=1, replica_groups=mesh['y'=8,'h'=2,'c'=2,'z'=4,'x'=4] {'y','c'}, dimensions={0} | all-to-all | bytes 229376 | tf_op jit(solution)/shard_map/all_to_all | solution.py:215
  61.0 0.4 shard_map.106
  61.4 10.1 %all_to_all.23.parts_ref = f32[16,8,128]{2,1,0:T(8,128)S(1)} all-to-all(f32[16,8,128]{2,1,0:T(8,128)S(1)} %get-tuple-element.21), channel_id=1, replica_groups=mesh['y'=8,'h'=2,'c'=2,'z'=4,'x'=4] {'z','x'}, dimensions={0} | all-to-all | bytes 131072 | tf_op jit(solution)/shard_map/all_to_all | solution.py:215
  71.5 0.7 %shard_map.107 = (f32[8,128]{1,0:T(8,128)}, f32[4,8]{1,0:T(4,128)}, f32[8,256]{1,0:T(8,128)}) custom-call(f32[16,8,128]{2,1,0:T(8,128)S(1)} %all_to_all.23.parts_ref, f32[8,128]{1,0:T(8,128)S(1)} %get-tuple-element.22.sets_ref, f32[8,256]{1,0:T(8,128)S(1)} %get-tuple-element.23.grads_ref), custom_call_target="tpu_custom_call" | custom-call | tf_op jit(solution)/shard_map/pallas_call | solution.py:252

commit v8 on v6

--- a/solution.py
+++ b/solution.py
@@ -243,7 +243,7 @@
         ],
         [VMEM],
     )(here(came))
-    parts = exchange(spread, TENSOR)
+    parts = exchange(spread, ("x", "z"))
     pair_scores, set_scores, source_grads = call(
         finish,
         [

time: 72.5 us -> 72.2 us (level)
  no operation moved by 1% of the time
where the time goes in v8:
time: 72.2 us; the launch traced here: 71.9 us
  blocking collectives  66.1 us (92%)
  Pallas kernels  5.16 us (7%)
    all_to_all x4, blocking collectives, exchange(): return lax.all_to_all(blocks, axes, 0, 0, tiled=True)  66.1 us
    pallas_call x1, Pallas kernels, local(): call(project, [pltpu.VMEM((RANKS, WIDTH, 2 * MINE * SLOTS), bf16), pltpu....  3.22 us

profile of v8, /device:TPU:1, one launch (start us, length us, event | category | flops | bytes accessed | tf_op | source)
XLA Modules:
  0.0 71.9 jit_solution(5418497500297653908)
XLA Ops:
  0.6 3.2 %shard_map.103 = (bf16[16,64,128]{2,1,0:T(8,128)(2,1)S(1)}, f32[2,64,128]{2,1,0:T(8,128)S(1)}, f32[32,8,640]{2,1,0:T(8,128)S(1)}, f32[32,8,128]{2,1,0:T(8,128)S(1)}, f32[32,8,128]{2,1,0:T(8,128)S(1)}) custom-call(bf16[1024,1792]{1,0:T(8,128)(2,1)} %refs_0_.1, bf16[1024,512]{1,0:T(8,128)(2,1)} %refs_1_.1, bf16[64,1792]{1,0:T(8,128)(2,1)} %bitcast.4, ...), custom_call_target="tpu_custom_call" | custom-call | tf_op jit(solution)/shard_map/pallas_call | solution.py:218
  3.9 19.7 %all_to_all.20.part_ref = bf16[16,64,128]{2,1,0:T(8,128)(2,1)S(1)} all-to-all(bf16[16,64,128]{2,1,0:T(8,128)(2,1)S(1)} %get-tuple-element.14), channel_id=1, replica_groups=mesh['y'=8,'h'=2,'c'=2,'z'=4,'x'=4] {'z','x'}, dimensions={0} | all-to-all | bytes 524288 | tf_op jit(solution)/shard_map/all_to_all | solution.py:211
  23.5 0.4 shard_map.104
  24.0 16.7 %all_to_all.21.got_ref = bf16[32,2,896]{2,1,0:T(2,128)(2,1)S(1)} all-to-all(bf16[32,2,896]{2,1,0:T(2,128)(2,1)S(1)} %shard_map.104), channel_id=1, replica_groups=mesh['y'=8,'h'=2,'c'=2,'z'=4,'x'=4] {'h','z','x'}, dimensions={0} | all-to-all | bytes 229376 | tf_op jit(solution)/shard_map/all_to_all | solution.py:211
  40.7 0.4 shard_map.105
  41.1 20.0 %all_to_all.22.came_ref = bf16[16,4,896]{2,1,0:T(4,128)(2,1)S(1)} all-to-all(bf16[16,4,896]{2,1,0:T(4,128)(2,1)S(1)} %shard_map.105), channel_id=1, replica_groups=mesh['y'=8,'h'=2,'c'=2,'z'=4,'x'=4] {'y','c'}, dimensions={0} | all-to-all | bytes 229376 | tf_op jit(solution)/shard_map/all_to_all | solution.py:211
  61.0 0.4 shard_map.106
  61.4 9.7 %all_to_all.23.parts_ref = f32[16,8,128]{2,1,0:T(8,128)S(1)} all-to-all(f32[16,8,128]{2,1,0:T(8,128)S(1)} %get-tuple-element.19), channel_id=1, replica_groups=mesh['y'=8,'h'=2,'c'=2,'z'=4,'x'=4] {'x','z'}, dimensions={0} | all-to-all | bytes 131072 | tf_op jit(solution)/shard_map/all_to_all | solution.py:211
  71.2 0.7 %shard_map.107 = (f32[8,128]{1,0:T(8,128)}, f32[4,8]{1,0:T(4,128)}, f32[8,256]{1,0:T(8,128)}) custom-call(f32[16,8,128]{2,1,0:T(8,128)S(1)} %all_to_all.23.parts_ref, f32[8,128]{1,0:T(8,128)S(1)} %get-tuple-element.20.sets_ref, f32[8,256]{1,0:T(8,128)S(1)} %get-tuple-element.21.grads_ref), custom_call_target="tpu_custom_call" | custom-call | tf_op jit(solution)/shard_map/pallas_call | solution.py:247

commit v9 on v7

--- a/solution.py
+++ b/solution.py
@@ -248,7 +248,7 @@
         ],
         [VMEM] * 2,
     )(here(came), here(fixed))
-    parts = exchange(spread, TENSOR)
+    parts = exchange(spread, ("x", "z"))
     pair_scores, set_scores, source_grads = call(
         finish,
         [

time: 72.5 us -> 72.1 us (level)
  no operation moved by 1% of the time
where the time goes in v9:
time: 72.1 us; the launch traced here: 71.9 us
  blocking collectives  66.1 us (92%)
  Pallas kernels  5.14 us (7%)
    all_to_all x4, blocking collectives, exchange(): return lax.all_to_all(blocks, axes, 0, 0, tiled=True)  66.1 us
    pallas_call x1, Pallas kernels, local(): call(project, [pltpu.VMEM((RANKS, WIDTH, 2 * MINE * SLOTS), bf16), pltpu....  3.22 us

profile of v9, /device:TPU:1, one launch (start us, length us, event | category | flops | bytes accessed | tf_op | source)
XLA Modules:
  0.0 71.9 jit_solution(17540924950718589034)
XLA Ops:
  0.6 3.2 %shard_map.103 = (bf16[16,64,128]{2,1,0:T(8,128)(2,1)S(1)}, bf16[128,512]{1,0:T(8,128)(2,1)S(1)}, f32[128,128]{1,0:T(8,128)S(1)}, f32[32,8,640]{2,1,0:T(8,128)S(...) custom-call(bf16[1024,1792]{1,0:T(8,128)(2,1)} %refs_0_.1, bf16[1024,512]{1,0:T(8,128)(2,1)} %refs_1_.1, ...), custom_call_target="tpu_custom_call" | custom-call | tf_op jit(solution)/shard_map/pallas_call | solution.py:222
  3.9 19.7 %all_to_all.20.part_ref = bf16[16,64,128]{2,1,0:T(8,128)(2,1)S(1)} all-to-all(bf16[16,64,128]{2,1,0:T(8,128)(2,1)S(1)} %get-tuple-element.15), channel_id=1, replica_groups=mesh['y'=8,'h'=2,'c'=2,'z'=4,'x'=4] {'z','x'}, dimensions={0} | all-to-all | bytes 524288 | tf_op jit(solution)/shard_map/all_to_all | solution.py:215
  23.5 0.4 shard_map.104
  23.9 16.7 %all_to_all.21.got_ref = bf16[32,2,896]{2,1,0:T(2,128)(2,1)S(1)} all-to-all(bf16[32,2,896]{2,1,0:T(2,128)(2,1)S(1)} %shard_map.104), channel_id=1, replica_groups=mesh['y'=8,'h'=2,'c'=2,'z'=4,'x'=4] {'h','z','x'}, dimensions={0} | all-to-all | bytes 229376 | tf_op jit(solution)/shard_map/all_to_all | solution.py:215
  40.7 0.4 shard_map.105
  41.0 20.0 %all_to_all.22.came_ref = bf16[16,4,896]{2,1,0:T(4,128)(2,1)S(1)} all-to-all(bf16[16,4,896]{2,1,0:T(4,128)(2,1)S(1)} %shard_map.105), channel_id=1, replica_groups=mesh['y'=8,'h'=2,'c'=2,'z'=4,'x'=4] {'y','c'}, dimensions={0} | all-to-all | bytes 229376 | tf_op jit(solution)/shard_map/all_to_all | solution.py:215
  61.0 0.4 shard_map.106
  61.4 9.7 %all_to_all.23.parts_ref = f32[16,8,128]{2,1,0:T(8,128)S(1)} all-to-all(f32[16,8,128]{2,1,0:T(8,128)S(1)} %get-tuple-element.21), channel_id=1, replica_groups=mesh['y'=8,'h'=2,'c'=2,'z'=4,'x'=4] {'x','z'}, dimensions={0} | all-to-all | bytes 131072 | tf_op jit(solution)/shard_map/all_to_all | solution.py:215
  71.1 0.7 %shard_map.107 = (f32[8,128]{1,0:T(8,128)}, f32[4,8]{1,0:T(4,128)}, f32[8,256]{1,0:T(8,128)}) custom-call(f32[16,8,128]{2,1,0:T(8,128)S(1)} %all_to_all.23.parts_ref, f32[8,128]{1,0:T(8,128)S(1)} %get-tuple-element.22.sets_ref, f32[8,256]{1,0:T(8,128)S(1)} %get-tuple-element.23.grads_ref), custom_call_target="tpu_custom_call" | custom-call | tf_op jit(solution)/shard_map/pallas_call | solution.py:252
